TPU v7x, 256 devices: a whole 4x4x8 slice. The times are simulated.
256 devices in a mesh: dp: 8 (over z), seq: 8 (over x_hi, y), tp: 4 (over x_lo, core).
Axes of the slice: x: 4 (x_hi: 2, x_lo: 2; x = x_hi * 2 + x_lo), y: 4, z: 8, core: 2. Of those that a mesh axis runs over, the one named last changes fastest.
Arguments:
- latent_query: bfloat16 [8, 4096, 2048], P('dp', ('seq', 'tp')), may hold values from -26 to 26
- latent_key: bfloat16 [8, 4096, 2048], P('dp', ('seq', 'tp')), may hold values from -26 to 26
- latent_value: bfloat16 [8, 4096, 2048], P('dp', ('seq', 'tp')), may hold values from -6 to 6
- out_grad: bfloat16 [8, 4096, 2048], P('dp', ('seq', 'tp')), may hold values from -384 to 384
- query_hidden: bfloat16 [8, 64, 3584], P('dp'), may hold values from -6 to 6
- cond_weight: bfloat16 [3584, 2, 2048], P(None, None, 'seq'), may hold values from -0.09375 to 0.09375
Outputs:
- grad_query: bfloat16 [8, 4096, 2048], P('dp', ('seq', 'tp'))
- grad_key: bfloat16 [8, 4096, 2048], P('dp', ('seq', 'tp'))
- grad_value: bfloat16 [8, 4096, 2048], P('dp', ('seq', 'tp'))
- grad_cond_weight: float32 [3584, 2, 2048], P(('dp', 'tp'), None, 'seq')
All inputs are finite; a program needn't handle non-finite values.
Results may differ from a plain program's by a relative error of at most 0.009.
Values may be sent and summed in bfloat16 or wider, within the bound.
A program may use at most 192 MiB of HBM per device.

v0:
```python
import jax
import jax.numpy as jnp
from jax import lax
from jax.sharding import PartitionSpec as P

HD = 128


def heads_first(matrix, head_count):
    return matrix.reshape(matrix.shape[0], head_count, HD).transpose(1, 0, 2)


def rows_back(matrix):
    return matrix.transpose(1, 0, 2).reshape(1, matrix.shape[1], matrix.shape[0] * matrix.shape[2])


def on_device(latent_query, latent_key, latent_value, out_grad, query_hidden, cond_weight):
    score_scale = HD ** (-0.5)
    queries, keys_in, values_in, grads_in = (
        lax.all_to_all(latent_query, "seq", split_axis=2, concat_axis=1, tiled=True),
        lax.all_to_all(latent_key, "seq", split_axis=2, concat_axis=1, tiled=True),
        lax.all_to_all(latent_value, "seq", split_axis=2, concat_axis=1, tiled=True),
        lax.all_to_all(out_grad, "seq", split_axis=2, concat_axis=1, tiled=True),
    )
    feat_width = cond_weight.shape[2]
    head_count = feat_width // HD
    hidden_rows = query_hidden[0]
    query_count = hidden_rows.shape[0]
    hidden_width = hidden_rows.shape[1]
    cond = jnp.dot(
        hidden_rows,
        cond_weight.reshape(hidden_width, 2 * feat_width),
        preferred_element_type=jnp.float32,
    )
    cond = cond.astype(jnp.bfloat16).reshape(query_count, 2, feat_width)
    row_total = queries.shape[1]
    keys_all, values_all = (
        lax.all_gather(keys_in, "tp", axis=1, tiled=True),
        lax.all_gather(values_in, "tp", axis=1, tiled=True),
    )
    key_full = heads_first(jnp.concatenate([keys_all[0], cond[:, 0]], 0), head_count)
    value_full = heads_first(jnp.concatenate([values_all[0], cond[:, 1]], 0), head_count)
    total_keys = key_full.shape[1]
    self_keys = keys_all.shape[1]
    block_rows = min(512, row_total)
    block_count = row_total // block_rows
    query_blocks = queries[0].reshape(block_count, block_rows, head_count, HD).transpose(0, 2, 1, 3)
    grad_blocks = grads_in[0].reshape(block_count, block_rows, head_count, HD).transpose(0, 2, 1, 3)

    def visit(totals, pair):
        key_acc, value_acc = totals
        query_block, grad_block = pair
        scores = (
            jnp.einsum("hqd,hkd->hqk", query_block, key_full, preferred_element_type=jnp.float32)
            * score_scale
        )
        row_max = jnp.max(scores, axis=2, keepdims=True)
        weights_exp = jnp.exp(scores - row_max)
        probs = weights_exp / jnp.sum(weights_exp, axis=2, keepdims=True)
        dprobs = jnp.einsum(
            "hqd,hkd->hqk", grad_block, value_full, preferred_element_type=jnp.float32
        )
        dot_sum = jnp.sum(probs * dprobs, axis=2, keepdims=True)
        dscores = (probs * (dprobs - dot_sum)).astype(jnp.bfloat16)
        probs_low = probs.astype(jnp.bfloat16)
        grad_q = (
            jnp.einsum("hqk,hkd->hqd", dscores, key_full, preferred_element_type=jnp.float32)
            * score_scale
        ).astype(jnp.bfloat16)
        key_acc = (
            key_acc
            + jnp.einsum("hqk,hqd->hkd", dscores, query_block, preferred_element_type=jnp.float32)
            * score_scale
        )
        value_acc = value_acc + jnp.einsum(
            "hqk,hqd->hkd", probs_low, grad_block, preferred_element_type=jnp.float32
        )
        return ((key_acc, value_acc), grad_q)

    empty = jnp.zeros((head_count, total_keys, HD), jnp.float32)
    (key_acc, value_acc), grad_q = lax.scan(visit, (empty, empty), (query_blocks, grad_blocks))
    key_self = rows_back(key_acc[:, :self_keys])
    value_self = rows_back(value_acc[:, :self_keys])
    key_owned, value_owned = (
        lax.psum_scatter(key_self, "tp", scatter_dimension=1, tiled=True),
        lax.psum_scatter(value_self, "tp", scatter_dimension=1, tiled=True),
    )
    grad_rows = grad_q.transpose(0, 2, 1, 3).reshape(1, row_total, feat_width)
    cond_key = key_acc[:, self_keys:].transpose(1, 0, 2).reshape(query_count, feat_width)
    cond_value = value_acc[:, self_keys:].transpose(1, 0, 2).reshape(query_count, feat_width)
    cond_grad = jnp.stack([cond_key, cond_value], 1).reshape(query_count, 2 * feat_width)
    out_query, out_key, out_value = (
        lax.all_to_all(grad_rows, "seq", split_axis=1, concat_axis=2, tiled=True),
        lax.all_to_all(
            key_owned.astype(jnp.bfloat16), "seq", split_axis=1, concat_axis=2, tiled=True
        ),
        lax.all_to_all(
            value_owned.astype(jnp.bfloat16), "seq", split_axis=1, concat_axis=2, tiled=True
        ),
    )
    hidden_exact = hidden_rows.astype(jnp.float32)
    groups = lax.axis_size("dp")
    lanes = lax.axis_size("tp")
    share = hidden_width // (groups * lanes)
    weight_part = lax.psum_scatter(
        jnp.dot(hidden_exact.T, cond_grad, precision=lax.Precision.HIGHEST).reshape(
            lax.axis_size(("dp", "tp")) * share, 2, feat_width
        ),
        ("dp", "tp"),
        scatter_dimension=0,
        tiled=True,
    )
    return (out_query, out_key, out_value, weight_part)


def solution(mesh):
    placed = (
        P("dp", ("seq", "tp"), None),
        P("dp", ("seq", "tp"), None),
        P("dp", ("seq", "tp"), None),
        P("dp", ("seq", "tp"), None),
        P("dp", None, None),
        P(None, None, "seq"),
    )
    return jax.shard_map(
        on_device,
        mesh=mesh,
        in_specs=placed,
        out_specs=(
            P("dp", ("seq", "tp"), None),
            P("dp", ("seq", "tp"), None),
            P("dp", ("seq", "tp"), None),
            P(("dp", "tp"), None, "seq"),
        ),
        check_vma=False,
    )
```

profile of v0, /device:TPU:1, one launch (start us, length us, event | category | flops | bytes accessed | tf_op | source)
XLA Modules:
  0.0 690.0 jit_solution(1208917480609452233)
XLA Ops:
  7.2 2.4 copy.98
  10.2 11.5 %reduce.1 = bf16[2048,128]{1,0:T(8,128)(2,1)S(1)} reduce(bf16[2048,1,128]{2,1,0:T(2,128)(2,1)S(1)} %bitcast.135, bf16[]{:T(256)} %broadcast.36), dimensions={1}, to_apply=%bitcast.79.reduce_sub_computation | reduce | bytes 1048578
  21.8 17.3 %all_to_all.120 = bf16[8,2,16384]{2,1,0:T(2,128)(2,1)S(1)} all-to-all(bf16[8,2,16384]{2,1,0:T(2,128)(2,1)S(1)} %reshape.55), channel_id=1, replica_groups=mesh['dp'=8,'seq'=8,'tp'=4] {'seq'}, dimensions={0} | all-to-all | bytes 1048576 | tf_op jit(solution)/shard_map/all_to_all | solution.py:21
  39.7 1.0 copy.99
  41.6 11.6 %reduce.3 = bf16[2048,128]{1,0:T(8,128)(2,1)S(1)} reduce(bf16[2048,1,128]{2,1,0:T(2,128)(2,1)S(1)} %bitcast.139, bf16[]{:T(256)} %broadcast.36), dimensions={1}, to_apply=%bitcast.83.reduce_sub_computation | reduce | bytes 1048578
  53.3 18.4 %all_to_all.121 = bf16[8,2,16384]{2,1,0:T(2,128)(2,1)S(1)} all-to-all(bf16[8,2,16384]{2,1,0:T(2,128)(2,1)S(1)} %reshape.59), channel_id=1, replica_groups=mesh['dp'=8,'seq'=8,'tp'=4] {'seq'}, dimensions={0} | all-to-all | bytes 1048576 | tf_op jit(solution)/shard_map/all_to_all | solution.py:22
  72.3 1.0 copy.106
  74.1 11.5 %reduce = bf16[2048,128]{1,0:T(8,128)(2,1)S(1)} reduce(bf16[2048,1,128]{2,1,0:T(2,128)(2,1)S(1)} %bitcast.140, bf16[]{:T(256)} %broadcast.36), dimensions={1}, to_apply=%bitcast.77.reduce_sub_computation | reduce | bytes 1048578
  85.6 0.9 reshape.53
  86.5 3.7 all-to-all-start
  90.2 4.4 copy.146
  95.4 11.5 %reduce.2 = bf16[2048,128]{1,0:T(8,128)(2,1)S(1)} reduce(bf16[2048,1,128]{2,1,0:T(2,128)(2,1)S(1)} %bitcast.141, bf16[]{:T(256)} %broadcast.36), dimensions={1}, to_apply=%bitcast.81.reduce_sub_computation | reduce | bytes 1048578
  106.9 0.9 reshape.57
  107.9 6.6 all-to-all-start.2
  114.6 2.8 convolution_convert_fusion
  118.6 0.9 reshape_squeeze.6
  119.5 3.6 all-to-all-done.2
  124.0 0.9 reshape_squeeze.7
  124.9 2.9 copy.100
  127.8 1.5 maximum_bitcast_fusion
  129.3 3.2 copy.111
  132.6 4.2 copy.107
  136.7 3.1 maximum_bitcast_fusion.1
  139.8 4.2 copy.113
  144.0 156.1 %while.15 = (s32[]{:T(128)}, f32[2,4160,128]{2,1,0:T(8,128)}, f32[2,4160,128]{2,1,0:T(8,128)}, bf16[2,2,512,128]{3,2,1,0:T(8,128)(2,1)}, bf16[2,2,512,128]{3,1,2...) while((s32[]{:T(128)}, f32[2,4160,128]{2,1,0:T(8,128)}, ...), condition=%wide.region_4.5_spmd.clone, body=%wide.region_0.4_spmd.clone.sunk | while | flops 5513563136 | bytes 191881408 | solution.py:81
  154.3 1.4 constant_dynamic-slice_fusion.4
  155.7 8.2 %fusion.46 = f32[2,512,4160]{1,2,0:T(8,128)} fusion(bf16[2,4160,128]{2,1,0:T(8,128)(2,1)S(1)} %get-tuple-element.234, bf16[1,2,512,128]{3,1,2,0:T(2,128)(2,1)S(1)} %get-tuple-element.203), kind=kOutput, calls=%fused_computation.19.clone.1 | convolution fusion | flops 1090519040 | bytes 19431424 | tf_op jit(solution)/shard_map/while/body/eval_jaxpr/hqd,hkd->hqk/dot_general | solution.py:54
  163.9 19.2 %fusion.47 = (f32[2,512]{1,0:T(2,128)S(1)}, f32[2,512,4160]{1,2,0:T(8,128)}) fusion(f32[2,512,4160]{1,2,0:T(8,128)} %fusion.46), kind=kOutput, calls=%fused_computation.34.clone.1 | output fusion | flops 17043520 | bytes 34082816 | tf_op jit(solution)/shard_map/while/body/eval_jaxpr/sub | solution.py:58
  183.1 10.3 %fusion.49 = f32[2,4160,128]{2,1,0:T(8,128)} fusion(f32[2,4160,128]{2,1,0:T(8,128)} %get-tuple-element.221, pred[]{:T(512)S(6)} %compare.3, bf16[1,2,512,128]{3,1,2,0:T(2,128)(2,1)S(1)} %get-tuple-element.206, f32[2,512,4160]{1,2,0:T(8,128)} %get-tuple-element.204, f32[2,512]{1,0:T(2,128)S(1)} %get-tuple-element.205), kind=kOutput, calls=%fused_computation.12.clone.1 | convolution fusion | flops 1101168640 | bytes 25825280 | tf_op jit(solution)/shard_map/while/body/eval_jaxpr/hqk,hqd->hkd/dot_general | solution.py:75
  193.4 11.4 %multiply_reduce_fusion.3 = (f32[2,512]{1,0:T(2,128)S(1)}, f32[2,512,4160]{1,2,0:T(8,128)}) fusion(f32[2,512,4160]{1,2,0:T(8,128)} %get-tuple-element.204, f32[2,512]{1,0:T(2,128)S(1)} %get-tuple-element.205, bf16[2,4160,128]{2,1,0:T(8,128)(2,1)} %get-tuple-element.236, bf16[1,2,512,128]{3,1,2,0:T(2,128)(2,1)S(1)} %get-tuple-element.206), kind=kOutput, calls=%fused_computation.2.clone.1 | convolution fusion | flops 1103297536 | bytes 36478976 | tf_op jit(solution)/shard_map/while/body/eval_jaxpr/hqd,hkd->hqk/dot_general | solution.py:60
  204.8 11.7 %multiply_convert_fusion.2 = bf16[2,512,4160]{1,2,0:T(8,128)(2,1)S(1)} fusion(f32[2,512,4160]{1,2,0:T(8,128)} %get-tuple-element.207, f32[2,512]{1,0:T(2,128)S(1)} %get-tuple-element.208, f32[2,512,4160]{1,2,0:T(8,128)} %get-tuple-element.204, f32[2,512]{1,0:T(2,128)S(1)} %get-tuple-element.205), kind=kLoop, calls=%fused_computation.1.clone.1 | loop fusion | flops 17039360 | bytes 42606592 | tf_op jit(solution)/shard_map/while/body/eval_jaxpr/convert_element_type | solution.py:64
  216.5 4.5 fusion.48
  221.0 3.6 fusion.50
  225.4 1.4 constant_dynamic-slice_fusion.4
  226.8 8.2 %fusion.46 = f32[2,512,4160]{1,2,0:T(8,128)} fusion(bf16[2,4160,128]{2,1,0:T(8,128)(2,1)S(1)} %get-tuple-element.234, bf16[1,2,512,128]{3,1,2,0:T(2,128)(2,1)S(1)} %get-tuple-element.203), kind=kOutput, calls=%fused_computation.19.clone.1 | convolution fusion | flops 1090519040 | bytes 19431424 | tf_op jit(solution)/shard_map/while/body/eval_jaxpr/hqd,hkd->hqk/dot_general | solution.py:54
  235.0 19.2 %fusion.47 = (f32[2,512]{1,0:T(2,128)S(1)}, f32[2,512,4160]{1,2,0:T(8,128)}) fusion(f32[2,512,4160]{1,2,0:T(8,128)} %fusion.46), kind=kOutput, calls=%fused_computation.34.clone.1 | output fusion | flops 17043520 | bytes 34082816 | tf_op jit(solution)/shard_map/while/body/eval_jaxpr/sub | solution.py:58
  254.2 11.5 %fusion.49 = f32[2,4160,128]{2,1,0:T(8,128)} fusion(f32[2,4160,128]{2,1,0:T(8,128)} %get-tuple-element.221, pred[]{:T(512)S(6)} %compare.3, bf16[1,2,512,128]{3,1,2,0:T(2,128)(2,1)S(1)} %get-tuple-element.206, f32[2,512,4160]{1,2,0:T(8,128)} %get-tuple-element.204, f32[2,512]{1,0:T(2,128)S(1)} %get-tuple-element.205), kind=kOutput, calls=%fused_computation.12.clone.1 | convolution fusion | flops 1101168640 | bytes 25825280 | tf_op jit(solution)/shard_map/while/body/eval_jaxpr/hqk,hqd->hkd/dot_general | solution.py:75
  265.7 11.4 %multiply_reduce_fusion.3 = (f32[2,512]{1,0:T(2,128)S(1)}, f32[2,512,4160]{1,2,0:T(8,128)}) fusion(f32[2,512,4160]{1,2,0:T(8,128)} %get-tuple-element.204, f32[2,512]{1,0:T(2,128)S(1)} %get-tuple-element.205, bf16[2,4160,128]{2,1,0:T(8,128)(2,1)} %get-tuple-element.236, bf16[1,2,512,128]{3,1,2,0:T(2,128)(2,1)S(1)} %get-tuple-element.206), kind=kOutput, calls=%fused_computation.2.clone.1 | convolution fusion | flops 1103297536 | bytes 36478976 | tf_op jit(solution)/shard_map/while/body/eval_jaxpr/hqd,hkd->hqk/dot_general | solution.py:60
  277.1 11.7 %multiply_convert_fusion.2 = bf16[2,512,4160]{1,2,0:T(8,128)(2,1)S(1)} fusion(f32[2,512,4160]{1,2,0:T(8,128)} %get-tuple-element.207, f32[2,512]{1,0:T(2,128)S(1)} %get-tuple-element.208, f32[2,512,4160]{1,2,0:T(8,128)} %get-tuple-element.204, f32[2,512]{1,0:T(2,128)S(1)} %get-tuple-element.205), kind=kLoop, calls=%fused_computation.1.clone.1 | loop fusion | flops 17039360 | bytes 42606592 | tf_op jit(solution)/shard_map/while/body/eval_jaxpr/convert_element_type | solution.py:64
  288.8 6.7 fusion.48
  295.5 3.6 fusion.50
  300.1 5.7 copy.117
  305.8 4.6 slice.26
  310.5 5.7 copy.120
  316.2 4.7 slice.27
  322.2 5.2 fusion.17
  327.4 11.7 %copy.126 = f32[3584,2,256]{2,1,0:T(2,128)} copy(f32[3584,2,256]{0,2,1:T(8,128)} %bitcast.120) | data formatting | bytes 14680064 | tf_op jit(solution)/shard_map/reshape | solution.py:106
  339.2 1.0 copy-done.6
  341.0 3.8 reduce.4
  345.7 3.5 all-to-all-start.4
  349.2 19.1 %reduce-scatter.3.cloned.1.call-done = f32[1,1024,256]{1,2,0:T(8,128)} async-done(((f32[1,4096,256]{1,2,0:T(8,128)}), f32[1,1024,256]{1,2,0:T(8,128)}) %reduce-scatter.3.cloned.1.call-update) | async-done | bytes 1048592 | tf_op jit(solution)/shard_map/reduce_scatter | solution.py:85
  368.3 1.3 convert_element_type.20
  370.5 3.8 reduce.5
  375.2 6.1 all-to-all-start.5
  381.3 42.3 %reduce-scatter.5.cloned.1.call-done = f32[1,1024,256]{1,2,0:T(8,128)} async-done(((f32[1,4096,256]{1,2,0:T(8,128)}), f32[1,1024,256]{1,2,0:T(8,128)}) %reduce-scatter.5.cloned.1.call-update) | async-done | bytes 1048592 | tf_op jit(solution)/shard_map/reduce_scatter | solution.py:86
  423.6 1.3 convert_element_type.21
  425.8 3.8 reduce.6
  429.6 0.9 reshape.65
  430.5 7.1 %all-to-all-start.6 = ((bf16[8,2,16384]{2,1,0:T(2,128)(2,1)}), bf16[8,2,16384]{2,1,0:T(2,128)(2,1)S(1)}, u32[]{:S(2)}, u32[]{:S(2)}) async-start(bf16[8,2,16384]{2,1,0:T(2,128)(2,1)} %reshape.65), calls=%async_computation.8 | async-start | bytes 1048576 | tf_op jit(solution)/shard_map/all_to_all | solution.py:97
  439.8 1.0 copy.127
  440.8 236.8 %all-reduce.3.cloned.1.call-done = f32[3584,2,256]{2,1,0:T(2,128)} async-done(((f32[3584,2,256]{2,1,0:T(2,128)}), f32[3584,2,256]{2,1,0:T(2,128)}) %all-reduce.3.cloned.1.call-update) | async-done | bytes 7340048
  677.6 1.6 constant_dynamic-slice_fusion.2
  680.1 1.0 copy.128
  682.0 1.0 copy.129
  (81 shorter events, 16.9 us)
Async XLA Ops:
  7.2 107.4 %copy-start = (bf16[1,64,3584]{2,1,0:T(8,128)(2,1)S(1)}, bf16[1,64,3584]{2,1,0:T(8,128)(2,1)}, u32[]{:S(2)}) copy-start(bf16[1,64,3584]{2,1,0:T(8,128)(2,1)} %param.12) | copy-start | bytes 1376260
  7.2 117.7 %all-gather.3.cloned.1.call-start = ((), (), s32[]{:S(2)}) async-start(), calls=%async_computation.9 | async-start | bytes 2621440 | tf_op jit(solution)/shard_map/all_gather | solution.py:38
  9.6 31.2 %copy-start.1 = (bf16[1,128,2048]{2,1,0:T(8,128)(2,1)S(1)}, bf16[1,128,2048]{2,1,0:T(8,128)(2,1)}, u32[]{:S(2)}) copy-start(bf16[1,128,2048]{2,1,0:T(8,128)(2,1)} %param.10) | copy-start | bytes 1572868
  40.7 91.8 %all-gather.5.cloned.1.call-start = ((), (), s32[]{:S(2)}) async-start(), calls=%async_computation.10 | async-start | bytes 2621440 | tf_op jit(solution)/shard_map/all_gather | solution.py:39
  41.6 31.8 %copy-start.2 = (bf16[1,128,2048]{2,1,0:T(8,128)(2,1)S(1)}, bf16[1,128,2048]{2,1,0:T(8,128)(2,1)}, u32[]{:S(2)}) copy-start(bf16[1,128,2048]{2,1,0:T(8,128)(2,1)} %param.8) | copy-start | bytes 1572868
  86.5 8.2 %copy-start.3 = (bf16[1,128,2048]{2,1,0:T(8,128)(2,1)S(1)}, bf16[1,128,2048]{2,1,0:T(8,128)(2,1)}, u32[]{:S(2)}) copy-start(bf16[1,128,2048]{2,1,0:T(8,128)(2,1)} %param.11) | copy-start | bytes 1572868
  86.5 21.4 %all-to-all-start = ((bf16[8,2,16384]{2,1,0:T(2,128)(2,1)}), bf16[8,2,16384]{2,1,0:T(2,128)(2,1)S(1)}, u32[]{:S(2)}, u32[]{:S(2)}) async-start(bf16[8,2,16384]{2,1,0:T(2,128)(2,1)} %reshape.53), calls=%async_computation | async-start | bytes 1048576 | tf_op jit(solution)/shard_map/all_to_all | solution.py:20
  107.9 15.3 %all-to-all-start.2 = ((bf16[8,2,16384]{2,1,0:T(2,128)(2,1)}), bf16[8,2,16384]{2,1,0:T(2,128)(2,1)S(1)}, u32[]{:S(2)}, u32[]{:S(2)}) async-start(bf16[8,2,16384]{2,1,0:T(2,128)(2,1)} %reshape.57), calls=%async_computation.2 | async-start | bytes 1048576 | tf_op jit(solution)/shard_map/all_to_all | solution.py:23
  114.5 253.8 %reduce-scatter.3.cloned.1.call-start = ((), (), s32[]{:S(2)}) async-start(), calls=%async_computation.11 | async-start | bytes 5242880 | tf_op jit(solution)/shard_map/reduce_scatter | solution.py:85
  216.5 4.5 copy-start.4
  224.6 0.8 copy-start.5
  288.8 6.7 copy-start.4
  299.1 0.8 copy-start.5
  310.5 113.1 %reduce-scatter.5.cloned.1.call-start = ((), (), s32[]{:S(2)}) async-start(), calls=%async_computation.12 | async-start | bytes 5242880 | tf_op jit(solution)/shard_map/reduce_scatter | solution.py:86
  320.9 356.6 %all-reduce.3.cloned.1.call-start = ((), (), s32[]{:S(2)}) async-start(), calls=%async_computation.13 | async-start | bytes 14680064
  339.1 1.0 copy-start.6
  345.7 29.5 %all-to-all-start.4 = ((bf16[8,2,16384]{2,1,0:T(2,128)(2,1)}), bf16[8,2,16384]{2,1,0:T(2,128)(2,1)S(1)}, u32[]{:S(2)}, u32[]{:S(2)}) async-start(bf16[8,2,16384]{2,1,0:T(2,128)(2,1)} %reshape.61), calls=%async_computation.4 | async-start | bytes 1048576 | tf_op jit(solution)/shard_map/all_to_all | solution.py:93
  374.3 63.4 %copy-start.7 = (u32[256]{0:T(256)S(1)}, u32[256]{0:T(256)}, u32[]{:S(2)}) copy-start(u32[256]{0:T(256)} %constant.31) | copy-start | bytes 3076
  375.2 55.3 %all-to-all-start.5 = ((bf16[8,2,16384]{2,1,0:T(2,128)(2,1)}), bf16[8,2,16384]{2,1,0:T(2,128)(2,1)S(1)}, u32[]{:S(2)}, u32[]{:S(2)}) async-start(bf16[8,2,16384]{2,1,0:T(2,128)(2,1)} %reshape.63), calls=%async_computation.6 | async-start | bytes 1048576 | tf_op jit(solution)/shard_map/all_to_all | solution.py:94
  430.5 250.6 %all-to-all-start.6 = ((bf16[8,2,16384]{2,1,0:T(2,128)(2,1)}), bf16[8,2,16384]{2,1,0:T(2,128)(2,1)S(1)}, u32[]{:S(2)}, u32[]{:S(2)}) async-start(bf16[8,2,16384]{2,1,0:T(2,128)(2,1)} %reshape.65), calls=%async_computation.8 | async-start | bytes 1048576 | tf_op jit(solution)/shard_map/all_to_all | solution.py:97
Sparse Core Ops, SparseCore 0:
  40.9 38.3 all-gather.2
  81.1 34.2 all-gather.4
  310.6 57.6 reduce-scatter.2
  370.9 52.7 reduce-scatter.4
  426.1 251.3 all-reduce.2
where the time goes:
time: 700 us; the launch traced here: 690 us
  waiting for transfers between devices  302 us (43%)
  other arithmetic  126 us (18%)
  matrix products  87.4 us (12%)
  local copies, waits for them, and re-layouts  85.4 us (12%)
  blocking collectives  35.6 us (5%)
  starting transfers between devices  27.2 us (4%)
  between operations  15.3 us (2%)
  loops' own time  10.6 us (2%)
    unnamed x6, waiting for transfers between devices  237 us
    unnamed x10, other arithmetic  57.5 us
    reduce_scatter x1, waiting for transfers between devices, on_device(): lax.psum_scatter(value_self, 'tp', scatter_dimension=1, tiled=True)  42.3 us
    sub x2, other arithmetic, visit(): weights_exp = jnp.exp(scores - row_max)  38.4 us
    unnamed x46, local copies, waits for them, and re-layouts  32.4 us
    convert_element_type x2, other arithmetic, visit(): dscores = (probs * (dprobs - dot_sum)).astype(jnp.bfloat16)  23.4 us
    dot_general x2, matrix products, visit(): jnp.einsum('hqd,hkd->hqk', grad_block, value_full, preferred_element_type...  22.8 us
    dot_general x2, matrix products, visit(): jnp.einsum('hqk,hqd->hkd', probs_low, grad_block, preferred_element_type=...  21.7 us
  transfers between devices with their start and end apart: 10, of which 4 were waited for; matrix products, arithmetic and copies ran while one was open for 16% of the time, Pallas kernels for 0%

commit v1 on v0

v1 whole, which is shorter than its diff:
```python
import jax
import jax.numpy as jnp
from jax import lax
from jax.experimental import pallas as pl
from jax.experimental.pallas import tpu as pltpu
from jax.sharding import PartitionSpec as P

HD = 128
MESH = pl.DeviceIdType.MESH
F32 = jnp.float32
BF16 = jnp.bfloat16
SCALE = HD ** (-0.5)
SCALE2 = SCALE * 1.4426950408889634
ROWS = 128
SLOTS = 16
QB = 1024
KT = 1024
KEYS = 4096
COND = 64
TILES = KEYS // KT
TILE_SLOTS = SLOTS // TILES
BLOCK_SLOTS = QB // ROWS
WINDOW = 512


def mm(a, b, ca, cb):
    return lax.dot_general(a, b, (((ca,), (cb,)), ((), ())), preferred_element_type=F32)


def gray(a):
    return a + (a // 2) * (1 - 2 * (a % 2))


def offset_of(slot):
    return gray(slot // 4), gray(slot % 4)


def rows_at(start, size):
    if isinstance(start, int):
        return pl.ds(start, size)
    return pl.ds(pl.multiple_of(start, 64), size)


def arrived(ref, sem):
    pltpu.make_async_copy(ref, ref, sem).wait()


def kernel(
    lq, lk, lv, og, hid, cw,
    dq_o, dk_o, dv_o, w_o,
    qb, gb, kb, vb, qt, gt, e_s, dp_s, m_s, ka, va, dqb,
    st, rx, fin, cwv, hida, c_st, c_rx, cga, prod,
    in_s, in_r, fw_s, fw_r, ex_s, ex_r, out_s, out_r,
    hid_s, hid_r, c1_s, c1_r, cg_s, cg_r, w_s, w_r, cw_sem,
):
    z = lax.axis_index("dp")
    seq = lax.axis_index("seq")
    tp = lax.axis_index("tp")
    x = (seq // 4) * 2 + tp // 2
    y = seq % 4
    core = tp % 2
    head = 2 * seq + tp // 2
    partner = {"tp": (tp // 2) * 2 + 1 - core}

    def chip(slot, sign):
        dx, dy = offset_of(slot)
        cx = (x + sign * dx + 4) % 4
        cy = (y + sign * dy + 4) % 4
        cseq = (cx // 2) * 4 + cy
        return {"seq": cseq, "tp": (cx % 2) * 2 + core}, 2 * cseq + cx % 2

    def feat(index):
        return pl.ds(pl.multiple_of(index * HD, HD), HD)

    barrier = pltpu.get_barrier_semaphore()

    def greet(slot, carry):
        device, _ = chip(slot, 1)
        pl.semaphore_signal(barrier, inc=1, device_id=device, device_id_type=MESH)
        return carry

    lax.fori_loop(1, SLOTS, greet, 0)
    pl.semaphore_signal(barrier, inc=1, device_id=partner, device_id_type=MESH)
    pl.semaphore_signal(barrier, inc=1, device_id={"tp": 3 - tp}, device_id_type=MESH)
    for dz in range(1, 8):
        pl.semaphore_signal(
            barrier, inc=1, device_id={"dp": (z + dz) % 8}, device_id_type=MESH
        )

    weights = pltpu.make_async_copy(
        cw.at[:, :, feat(tp // 2)], cwv, cw_sem
    )
    weights.start()
    for a, (src, dst) in enumerate(((lq, qb), (og, gb))):
        pltpu.make_async_copy(src.at[0, :, feat(head)], dst.at[pl.ds(0, ROWS)], in_r.at[a, 0]).start()
    for a, (src, dst) in enumerate(((lk, kb), (lv, vb))):
        pltpu.make_async_copy(
            src.at[0, :, feat(head)], dst.at[rows_at(core * ROWS, ROWS)], in_r.at[2 + a, 0]
        ).start()

    pl.semaphore_wait(barrier, 24)

    def in_copy(a, src, dst, dst_start, slot):
        device, there = chip(slot, 1)
        return pltpu.make_async_remote_copy(
            src_ref=src.at[0, :, feat(there)],
            dst_ref=dst.at[rows_at(dst_start, ROWS)],
            send_sem=in_s.at[a, slot],
            recv_sem=in_r.at[a, slot],
            device_id=device,
            device_id_type=MESH,
        )

    def send_q(slot, carry):
        in_copy(0, lq, qb, slot * ROWS, slot).start()
        in_copy(1, og, gb, slot * ROWS, slot).start()
        return carry

    def send_k(slot, carry):
        in_copy(2, lk, kb, slot * 2 * ROWS + core * ROWS, slot).start()
        in_copy(3, lv, vb, slot * 2 * ROWS + core * ROWS, slot).start()
        return carry

    lax.fori_loop(1, TILE_SLOTS, send_k, 0)
    lax.fori_loop(1, BLOCK_SLOTS, send_q, 0)
    lax.fori_loop(TILE_SLOTS, SLOTS, send_k, 0)
    lax.fori_loop(BLOCK_SLOTS, SLOTS, send_q, 0)

    def window(zz):
        return pl.ds(pl.multiple_of((7 * zz // 2) * HD, HD), WINDOW)

    for dz in range(1, 8):
        there = (z + dz) % 8
        pltpu.make_async_remote_copy(
            src_ref=hid.at[0, :, window(there)],
            dst_ref=hida.at[dz],
            send_sem=hid_s.at[dz],
            recv_sem=hid_r.at[dz],
            device_id={"dp": there},
            device_id_type=MESH,
        ).start()
    hida[0] = hid[0, :, window(z)]

    weights.wait()

    def cond_step(i, sums):
        r = pl.multiple_of(i * 512, 512)
        rows = hid[0, :, pl.ds(r, 512)]
        return (
            sums[0] + mm(rows, cwv[pl.ds(r, 512), 0, :], 1, 0),
            sums[1] + mm(rows, cwv[pl.ds(r, 512), 1, :], 1, 0),
        )

    nothing = jnp.zeros((COND, HD), F32)
    cond_k, cond_v = lax.fori_loop(0, 7, cond_step, (nothing, nothing))
    kb[pl.ds(KEYS, COND), :] = cond_k.astype(BF16)
    vb[pl.ds(KEYS, COND), :] = cond_v.astype(BF16)
    ka[...] = jnp.zeros_like(ka)
    va[...] = jnp.zeros_like(va)

    def take_queries(block):
        def wait_q(slot, carry):
            for a, dst in enumerate((qb, gb)):
                arrived(dst.at[rows_at(slot * ROWS, ROWS)], in_r.at[a, slot])
            return carry

        lax.fori_loop(block * BLOCK_SLOTS, (block + 1) * BLOCK_SLOTS, wait_q, 0)
        qt[...] = qb[pl.ds(block * QB, QB), :].T
        gt[...] = gb[pl.ds(block * QB, QB), :].T

    def take_keys(tile):
        def wait_k(i, carry):
            slot = tile * TILE_SLOTS + i
            for a, dst in enumerate((kb, vb)):
                mine = dst.at[rows_at(slot * 2 * ROWS + core * ROWS, ROWS)]
                arrived(mine, in_r.at[2 + a, slot])
                pltpu.make_async_remote_copy(
                    src_ref=mine,
                    dst_ref=mine,
                    send_sem=fw_s.at[a, slot],
                    recv_sem=fw_r.at[a, slot],
                    device_id=partner,
                    device_id_type=MESH,
                ).start()
            return carry

        def wait_f(i, carry):
            slot = tile * TILE_SLOTS + i
            for a, dst in enumerate((kb, vb)):
                arrived(dst.at[rows_at(slot * 2 * ROWS + (1 - core) * ROWS, ROWS)], fw_r.at[a, slot])
            return carry

        lax.fori_loop(0, TILE_SLOTS, wait_k, 0)
        lax.fori_loop(0, TILE_SLOTS, wait_f, 0)

    def forward(tile, stats, start, size):
        top, total, dots = stats
        keys = rows_at(start, size)
        scores = mm(kb[keys, :], qt[...], 1, 0)
        dprobs = mm(vb[keys, :], gt[...], 1, 0)
        top_new = jnp.maximum(top, jnp.max(scores, axis=0, keepdims=True) * SCALE2)
        e = jnp.exp2(scores * SCALE2 - top_new)
        shrink = jnp.exp2(top - top_new)
        total = total * shrink + jnp.sum(e, axis=0, keepdims=True)
        dots = dots * shrink + jnp.sum(e * dprobs, axis=0, keepdims=True)
        e_s[keys, :] = e.astype(BF16)
        dp_s[keys, :] = dprobs
        m_s[pl.ds(tile, 1), :] = top_new
        return top_new, total, dots

    def backward(tile, dq, stats, start, size):
        top, inverse, mean = stats
        keys = rows_at(start, size)
        factor = jnp.exp2(m_s[pl.ds(tile, 1), :] - top) * inverse
        grads = (gt[...].astype(F32) * factor).astype(BF16)
        queries = (qt[...].astype(F32) * (factor * SCALE)).astype(BF16)
        e = e_s[keys, :]
        ds = (e.astype(F32) * (dp_s[keys, :] - mean)).astype(BF16)
        va[keys, :] += mm(e, grads, 1, 1)
        ka[keys, :] += mm(ds, queries, 1, 1)
        return dq + mm(kb[keys, :], ds, 0, 0) * (factor * SCALE)

    def forward_all(block):
        low = jnp.full((1, QB), -1e30, F32)
        zero = jnp.zeros((1, QB), F32)

        def step(tile, stats):
            if block == 0:
                take_keys(tile)
            return forward(tile, stats, tile * KT, KT)

        stats = forward(TILES, (low, zero, zero), KEYS, COND)
        top, total, dots = lax.fori_loop(0, TILES, step, stats)
        inverse = 1.0 / total
        return top, inverse, dots * inverse

    def out_copy(a, src, dst, slot):
        device, _ = chip(slot, -1)
        return pltpu.make_async_remote_copy(
            src_ref=src,
            dst_ref=dst.at[0, :, feat(head)],
            send_sem=out_s.at[a, slot],
            recv_sem=out_r.at[a, slot],
            device_id=device,
            device_id_type=MESH,
        )

    def send_out(a, src, dst, slot):
        @pl.when(slot > 0)
        def _():
            out_copy(a, src, dst, slot).start()

        @pl.when(slot == 0)
        def _():
            pltpu.make_async_copy(src, dst.at[0, :, feat(head)], out_r.at[a, 0]).start()

    def send_dq(block, dq):
        dqb[pl.ds(block * QB, QB), :] = dq.T.astype(BF16)

        def one(slot, carry):
            send_out(0, dqb.at[rows_at(slot * ROWS, ROWS)], dq_o, slot)
            return carry

        lax.fori_loop(block * BLOCK_SLOTS, (block + 1) * BLOCK_SLOTS, one, 0)

    empty = jnp.zeros((HD, QB), F32)

    take_queries(0)
    stats = forward_all(0)
    dq = backward(TILES, empty, stats, KEYS, COND)
    dq = lax.fori_loop(0, TILES, lambda t, d: backward(t, d, stats, t * KT, KT), dq)
    send_dq(0, dq)

    take_queries(1)
    stats = forward_all(1)
    dq = backward(TILES, empty, stats, KEYS, COND)

    @pl.when(core == 0)
    def _():
        c_st[...] = va[pl.ds(KEYS, COND), :].astype(BF16)

    @pl.when(core == 1)
    def _():
        c_st[...] = ka[pl.ds(KEYS, COND), :].astype(BF16)

    pltpu.make_async_remote_copy(
        src_ref=c_st, dst_ref=c_rx, send_sem=c1_s, recv_sem=c1_r, device_id=partner, device_id_type=MESH
    ).start()

    def cond_sum():
        arrived(c_rx, c1_r)

        @pl.when(core == 0)
        def _():
            cga[0] = (ka[pl.ds(KEYS, COND), :] + c_rx[...].astype(F32)).astype(BF16)

        @pl.when(core == 1)
        def _():
            cga[0] = (va[pl.ds(KEYS, COND), :] + c_rx[...].astype(F32)).astype(BF16)

        for dz in range(1, 8):
            pltpu.make_async_remote_copy(
                src_ref=cga.at[0],
                dst_ref=cga.at[dz],
                send_sem=cg_s.at[dz],
                recv_sem=cg_r.at[dz],
                device_id={"dp": (z + dz) % 8},
                device_id_type=MESH,
            ).start()

    def part_copy(dt):
        owner = (tp + dt) % 4
        return pltpu.make_async_remote_copy(
            src_ref=prod.at[pl.ds(pl.multiple_of((z % 2) * 64 + owner * 112, 16), 112)],
            dst_ref=w_o.at[tp],
            send_sem=w_s.at[dt],
            recv_sem=w_r.at[dt],
            device_id={"tp": owner},
            device_id_type=MESH,
        )

    def cond_product():
        for dz in range(1, 8):
            arrived(hida.at[dz], hid_r.at[dz])
            arrived(cga.at[dz], cg_r.at[dz])
        prod[...] = mm(
            hida[...].reshape(8 * COND, WINDOW), cga[...].reshape(8 * COND, HD), 0, 0
        )
        for dt in range(1, 4):
            part_copy(dt).start()
        pltpu.make_async_copy(
            prod.at[pl.ds(pl.multiple_of((z % 2) * 64 + tp * 112, 16), 112)], w_o.at[tp], w_r.at[0]
        ).start()

    def tile_slots(tile):
        return pl.ds(pl.multiple_of(tile * TILE_SLOTS, TILE_SLOTS), TILE_SLOTS)

    def swap(tile):
        for i in range(TILE_SLOTS):
            slot = tile * TILE_SLOTS + i
            theirs = rows_at(slot * 2 * ROWS + (1 - core) * ROWS, ROWS)
            st[0, slot] = ka[theirs, :].astype(BF16)
            st[1, slot] = va[theirs, :].astype(BF16)
        for a in range(2):
            pltpu.make_async_remote_copy(
                src_ref=st.at[a, tile_slots(tile)],
                dst_ref=rx.at[a, tile_slots(tile)],
                send_sem=ex_s.at[a, tile],
                recv_sem=ex_r.at[a, tile],
                device_id=partner,
                device_id_type=MESH,
            ).start()

    def finish(tile):
        for a in range(2):
            arrived(rx.at[a, tile_slots(tile)], ex_r.at[a, tile])
        for i in range(TILE_SLOTS):
            slot = tile * TILE_SLOTS + i
            mine = rows_at(slot * 2 * ROWS + core * ROWS, ROWS)
            for a, (acc, dst) in enumerate(((ka, dk_o), (va, dv_o))):
                fin[a, slot] = (acc[mine, :] + rx[a, slot].astype(F32)).astype(BF16)
                send_out(1 + a, fin.at[a, slot], dst, slot)

    def last(i, d):
        tile = TILES - 1 - i
        d = backward(tile, d, stats, tile * KT, KT)
        swap(tile)

        @pl.when(i > 0)
        def _():
            finish(tile + 1)

        @pl.when(i == 0)
        def _():
            cond_sum()

        @pl.when(i == TILES - 2)
        def _():
            cond_product()

        return d

    dq = lax.fori_loop(0, TILES, last, dq)
    send_dq(1, dq)
    finish(0)

    def drain(slot, carry):
        for a, dst in enumerate((dq_o, dk_o, dv_o)):
            arrived(dst.at[0, :, feat(0)], out_r.at[a, slot])
        return carry

    def drain_sends(slot, carry):
        for a in range(4):
            arrived(qb.at[pl.ds(0, ROWS)], in_s.at[a, slot])
        for a in range(3):
            arrived(dqb.at[pl.ds(0, ROWS)], out_s.at[a, slot])
        return carry

    def drain_forwards(slot, carry):
        for a in range(2):
            arrived(kb.at[pl.ds(0, ROWS)], fw_s.at[a, slot])
        return carry

    lax.fori_loop(0, SLOTS, drain_forwards, 0)
    lax.fori_loop(1, SLOTS, drain_sends, 0)
    for tile in range(TILES):
        for a in range(2):
            arrived(st.at[a, pl.ds(tile * TILE_SLOTS, TILE_SLOTS)], ex_s.at[a, tile])
    arrived(c_st, c1_s)
    for dz in range(1, 8):
        arrived(hida.at[dz], hid_s.at[dz])
        arrived(cga.at[0], cg_s.at[dz])
    for dt in range(4):
        if dt:
            arrived(prod.at[pl.ds(0, 112)], w_s.at[dt])
        arrived(w_o.at[0], w_r.at[dt])
    lax.fori_loop(0, SLOTS, drain, 0)


def on_device(latent_query, latent_key, latent_value, out_grad, query_hidden, cond_weight):
    anywhere = pl.BlockSpec(memory_space=pl.ANY)
    token = jax.ShapeDtypeStruct(latent_query.shape, BF16)
    dma = pltpu.SemaphoreType.DMA
    total_keys = KEYS + COND
    grads = pl.pallas_call(
        kernel,
        name="attention_backward",
        out_shape=(token, token, token, jax.ShapeDtypeStruct((4, 112, HD), F32)),
        in_specs=[anywhere] * 4 + [pl.BlockSpec(memory_space=pltpu.VMEM), anywhere],
        out_specs=(anywhere,) * 4,
        scratch_shapes=[
            pltpu.VMEM((2 * QB, HD), BF16),
            pltpu.VMEM((2 * QB, HD), BF16),
            pltpu.VMEM((total_keys, HD), BF16),
            pltpu.VMEM((total_keys, HD), BF16),
            pltpu.VMEM((HD, QB), BF16),
            pltpu.VMEM((HD, QB), BF16),
            pltpu.VMEM((total_keys, QB), BF16),
            pltpu.VMEM((total_keys, QB), F32),
            pltpu.VMEM((8, QB), F32),
            pltpu.VMEM((total_keys, HD), F32),
            pltpu.VMEM((total_keys, HD), F32),
            pltpu.VMEM((2 * QB, HD), BF16),
            pltpu.VMEM((2, SLOTS, ROWS, HD), BF16),
            pltpu.VMEM((2, SLOTS, ROWS, HD), BF16),
            pltpu.VMEM((2, SLOTS, ROWS, HD), BF16),
            pltpu.VMEM((cond_weight.shape[0], 2, HD), BF16),
            pltpu.VMEM((8, COND, WINDOW), BF16),
            pltpu.VMEM((COND, HD), BF16),
            pltpu.VMEM((COND, HD), BF16),
            pltpu.VMEM((8, COND, HD), BF16),
            pltpu.VMEM((WINDOW, HD), F32),
            dma((4, SLOTS)), dma((4, SLOTS)),
            dma((2, SLOTS)), dma((2, SLOTS)),
            dma((2, TILES)), dma((2, TILES)),
            dma((3, SLOTS)), dma((3, SLOTS)),
            dma((8,)), dma((8,)),
            dma, dma,
            dma((8,)), dma((8,)),
            dma((4,)), dma((4,)),
            dma,
        ],
        compiler_params=pltpu.CompilerParams(
            collective_id=0, has_side_effects=True, vmem_limit_bytes=60 << 20
        ),
    )(latent_query, latent_key, latent_value, out_grad, query_hidden, cond_weight)
    out_query, out_key, out_value, parts = grads
    weight = parts.reshape(2, 2, 112, HD).transpose(2, 1, 0, 3).reshape(112, 2, 2 * HD)
    return (out_query, out_key, out_value, weight)


def solution(mesh):
    placed = (
        P("dp", ("seq", "tp"), None),
        P("dp", ("seq", "tp"), None),
        P("dp", ("seq", "tp"), None),
        P("dp", ("seq", "tp"), None),
        P("dp", None, None),
        P(None, None, "seq"),
    )
    return jax.shard_map(
        on_device,
        mesh=mesh,
        in_specs=placed,
        out_specs=(
            P("dp", ("seq", "tp"), None),
            P("dp", ("seq", "tp"), None),
            P("dp", ("seq", "tp"), None),
            P(("dp", "tp"), None, "seq"),
        ),
        check_vma=False,
    )
```

time: 700 us -> 98.7 us (0.14); the launches traced: 690 us -> 98.4 us
  waiting for transfers between devices: 302 us -> 0 us
  other arithmetic: 126 us -> 0 us
  Pallas kernels: 0 us -> 90.1 us
  matrix products: 87.4 us -> 0 us
  local copies, waits for them, and re-layouts: 85.4 us -> 7.71 us
  blocking collectives: 35.6 us -> 0 us
  starting transfers between devices: 27.2 us -> 0 us
  between operations: 15.3 us -> 0.64 us
  loops' own time: 10.6 us -> 0 us
    unnamed x6 -> x0, waiting for transfers between devices: 237 us -> none
    pallas_call x0 -> x1, Pallas kernels: none -> 90.1 us  [on_device(): pl.pallas_call(kernel, name='attention_backward', out_shape=(token, token...]
    dot_general x12 -> x0, matrix products: 87.4 us -> none  [the longest x2 22.8 us: visit(): jnp.einsum('hqd,hkd->hqk', grad_block, value_full, preferred_element_type...]
    reduce_scatter x2 -> x0, waiting for transfers between devices: 61.4 us -> none  [the longest x1 42.3 us: on_device(): lax.psum_scatter(value_self, 'tp', scatter_dimension=1, tiled=True)]
    unnamed x10 -> x0, other arithmetic: 57.5 us -> none
    sub x2 -> x0, other arithmetic: 38.4 us -> none  [visit(): weights_exp = jnp.exp(scores - row_max)]
    all_to_all x2 -> x0, blocking collectives: 35.6 us -> none  [the longest x1 18.4 us: on_device(): lax.all_to_all(latent_value, 'seq', split_axis=2, concat_axis=1, tiled=True)]
    all_to_all x5 -> x0, starting transfers between devices: 27 us -> none  [the longest x1 7.09 us: on_device(): lax.all_to_all(value_owned.astype(jnp.bfloat16), 'seq', split_axis=1, con...]
  transfers between devices with their start and end apart: 10 -> 0, of which waited for: 4 -> 0; matrix products, arithmetic and copies ran while one was open for 16% -> 0% of each run, Pallas kernels for 0% -> 0%
where the time goes in v1:
time: 98.7 us; the launch traced here: 98.4 us
  Pallas kernels  90.1 us (91%)
  local copies, waits for them, and re-layouts  7.71 us (8%)
    pallas_call x1, Pallas kernels, on_device(): pl.pallas_call(kernel, name='attention_backward', out_shape=(token, token...  90.1 us
    unnamed x3, local copies, waits for them, and re-layouts  5.64 us

profile of v1, /device:TPU:1, one launch (start us, length us, event | category | flops | bytes accessed | tf_op | source)
XLA Modules:
  0.0 98.4 jit_solution(12936638907476876735)
XLA Ops:
  0.6 90.1 %attention_backward.1 = (bf16[1,128,2048]{2,1,0:T(8,128)(2,1)}, bf16[1,128,2048]{2,1,0:T(8,128)(2,1)}, bf16[1,128,2048]{2,1,0:T(8,128)(2,1)}, f32[4,112,128]{2,1,0:T(8,128)}) custom-call(bf16[1,128,2048]{2,1,0:T(8,128)(2,1)} %lq.1, bf16[1,128,2048]{2,1,0:T(8,128)(2,1)} %lk.1, bf16[1,128,2048]{2,1,0:T(8,128)(2,1)} %lv.1, bf16[1,128,2048]{2,1,0:T(8,128)(2,1)} %og.1, ...), custom_call_target="tpu_custom_call" | custom-call | tf_op jit(solution)/shard_map/attention_backward/pallas_call | solution.py:425
  90.7 1.1 %copy.10 = f32[112,2,2,128]{3,2,1,0:T(2,128)S(1)} copy(f32[112,2,2,128]{3,0,1,2:T(8,128)} %bitcast.3) | data formatting | bytes 458752 | tf_op jit(solution)/shard_map/transpose | solution.py:468
  91.8 1.0 reshape.15
  92.8 1.9 %copy.14 = bf16[1,128,2048]{2,1,0:T(8,128)(2,1)} copy(bf16[1,128,2048]{2,1,0:T(8,128)(2,1)} %get-tuple-element.16) | data formatting | bytes 1048576
  94.7 1.9 %copy.15 = bf16[1,128,2048]{2,1,0:T(8,128)(2,1)} copy(bf16[1,128,2048]{2,1,0:T(8,128)(2,1)} %get-tuple-element.17) | data formatting | bytes 1048576
  96.6 1.9 %copy.16 = bf16[1,128,2048]{2,1,0:T(8,128)(2,1)} copy(bf16[1,128,2048]{2,1,0:T(8,128)(2,1)} %get-tuple-element.18) | data formatting | bytes 1048576

commit v2 on v1

v2 whole, which is shorter than its diff:
```python
import jax
import jax.numpy as jnp
from jax import lax
from jax.experimental import pallas as pl
from jax.experimental.pallas import tpu as pltpu
from jax.sharding import PartitionSpec as P

HD = 128
MESH = pl.DeviceIdType.MESH
F32 = jnp.float32
BF16 = jnp.bfloat16
SCALE = HD ** (-0.5)
SCALE2 = SCALE * 1.4426950408889634
ROWS = 128
SLOTS = 16
QB = 1024
KT = 512
BT = 2 * KT
KEYS = 4096
COND = 64
TILES = KEYS // KT
TILE_SLOTS = SLOTS // TILES
BACK_TILES = KEYS // BT
BACK_SLOTS = SLOTS // BACK_TILES
HALF_SLOTS = QB // ROWS
GROUP = 4
WINDOW = 512


def mm(a, b, ca, cb):
    return lax.dot_general(a, b, (((ca,), (cb,)), ((), ())), preferred_element_type=F32)


def offset_of(slot):
    return slot % 4, (slot % 4 + slot // 4) % 4


def rows_at(start, size):
    if isinstance(start, int):
        return pl.ds(start, size)
    return pl.ds(pl.multiple_of(start, 64), size)


def arrived(ref, sem):
    pltpu.make_async_copy(ref, ref, sem).wait()


def kernel(
    lq, lk, lv, og, hid, cw,
    dq_o, dk_o, dv_o, w_o,
    qb, gb, kb, vb, qt, gt, qi, gi, e_s, dp_s, m_s, ka, va, dqa, dqb,
    st, rx, fin, cwv, hida, c_st, c_rx, cga, prod,
    in_s, q_r, k_r, fw_s, fw_r, ex_s, ex_r, out_s, out_r,
    hid_s, hid_r, c1_s, c1_r, cg_s, cg_r, w_s, w_r, cw_sem,
):
    z = lax.axis_index("dp")
    seq = lax.axis_index("seq")
    tp = lax.axis_index("tp")
    x = (seq // 4) * 2 + tp // 2
    y = seq % 4
    core = tp % 2
    head = 2 * seq + tp // 2
    partner = {"tp": (tp // 2) * 2 + 1 - core}

    def chip(slot, sign):
        dx, dy = offset_of(slot)
        cx = (x + sign * dx + 4) % 4
        cy = (y + sign * dy + 4) % 4
        cseq = (cx // 2) * 4 + cy
        return {"seq": cseq, "tp": (cx % 2) * 2 + core}, 2 * cseq + cx % 2

    def feat(index):
        return pl.ds(pl.multiple_of(index * HD, HD), HD)

    barrier = pltpu.get_barrier_semaphore()

    def greet(slot, carry):
        device, _ = chip(slot, 1)
        pl.semaphore_signal(barrier, inc=1, device_id=device, device_id_type=MESH)
        return carry

    lax.fori_loop(1, SLOTS, greet, 0)
    pl.semaphore_signal(barrier, inc=1, device_id=partner, device_id_type=MESH)
    pl.semaphore_signal(barrier, inc=1, device_id={"tp": 3 - tp}, device_id_type=MESH)
    for dz in range(1, 8):
        pl.semaphore_signal(
            barrier, inc=1, device_id={"dp": (z + dz) % 8}, device_id_type=MESH
        )

    weights = pltpu.make_async_copy(
        cw.at[:, :, feat(tp // 2)], cwv, cw_sem
    )
    weights.start()
    for a, (src, dst) in enumerate(((lq, qb), (og, gb))):
        pltpu.make_async_copy(src.at[0, :, feat(head)], dst.at[pl.ds(0, ROWS)], q_r.at[a, 0]).start()
    for a, (src, dst) in enumerate(((lk, kb), (lv, vb))):
        pltpu.make_async_copy(
            src.at[0, :, feat(head)], dst.at[rows_at(core * ROWS, ROWS)], k_r.at[a, 0]
        ).start()

    with jax.named_scope("barrier"):
        pl.semaphore_wait(barrier, 24)

    def in_copy(a, src, dst, dst_start, slot, arrival):
        device, there = chip(slot, 1)
        return pltpu.make_async_remote_copy(
            src_ref=src.at[0, :, feat(there)],
            dst_ref=dst.at[rows_at(dst_start, ROWS)],
            send_sem=in_s.at[a],
            recv_sem=arrival,
            device_id=device,
            device_id_type=MESH,
        )

    def send_q(slot, carry):
        for a, (src, dst) in enumerate(((lq, qb), (og, gb))):
            in_copy(a, src, dst, slot * ROWS, slot, q_r.at[a, slot // GROUP]).start()
        return carry

    def send_k(slot, carry):
        row = slot * 2 * ROWS + core * ROWS
        for a, (src, dst) in enumerate(((lk, kb), (lv, vb))):
            in_copy(2 + a, src, dst, row, slot, k_r.at[a, slot // TILE_SLOTS]).start()
        return carry

    with jax.named_scope("send_inputs"):
        lax.fori_loop(1, HALF_SLOTS, send_q, 0)
        lax.fori_loop(1, 4, send_k, 0)

    def window(zz):
        return pl.ds(pl.multiple_of((7 * zz // 2) * HD, HD), WINDOW)

    for dz in range(1, 8):
        there = (z + dz) % 8
        pltpu.make_async_remote_copy(
            src_ref=hid.at[0, :, window(there)],
            dst_ref=hida.at[dz],
            send_sem=hid_s,
            recv_sem=hid_r,
            device_id={"dp": there},
            device_id_type=MESH,
        ).start()
    hida[0] = hid[0, :, window(z)]

    weights.wait()

    def cond_step(i, sums):
        r = pl.multiple_of(i * 512, 512)
        rows = hid[0, :, pl.ds(r, 512)]
        return (
            sums[0] + mm(rows, cwv[pl.ds(r, 512), 0, :], 1, 0),
            sums[1] + mm(rows, cwv[pl.ds(r, 512), 1, :], 1, 0),
        )

    nothing = jnp.zeros((COND, HD), F32)
    with jax.named_scope("condition_keys"):
        cond_k, cond_v = lax.fori_loop(0, 7, cond_step, (nothing, nothing))
    kb[pl.ds(KEYS, COND), :] = cond_k.astype(BF16)
    vb[pl.ds(KEYS, COND), :] = cond_v.astype(BF16)

    def take_queries(half):
        for group in (2 * half, 2 * half + 1):
            with jax.named_scope("wait_queries"):
                for a, dst in enumerate((qb, gb)):
                    arrived(dst.at[pl.ds(group * GROUP * ROWS, GROUP * ROWS)], q_r.at[a, group])
        qt[...] = qb[pl.ds(half * QB, QB), :].T
        gt[...] = gb[pl.ds(half * QB, QB), :].T
        dqa[...] = jnp.zeros_like(dqa)

    def pass_keys(tile):
        with jax.named_scope("wait_keys"):
            for a, dst in enumerate((kb, vb)):
                arrived(dst.at[pl.ds(0, TILE_SLOTS * ROWS)], k_r.at[a, tile])
        for i in range(TILE_SLOTS):
            for a, dst in enumerate((kb, vb)):
                mine = dst.at[rows_at((tile * TILE_SLOTS + i) * 2 * ROWS + core * ROWS, ROWS)]
                pltpu.make_async_remote_copy(
                    src_ref=mine,
                    dst_ref=mine,
                    send_sem=fw_s.at[a],
                    recv_sem=fw_r.at[a, tile],
                    device_id=partner,
                    device_id_type=MESH,
                ).start()

    def take_keys(tile):
        with jax.named_scope("wait_partner_keys"):
            for a, dst in enumerate((kb, vb)):
                arrived(dst.at[pl.ds(0, TILE_SLOTS * ROWS)], fw_r.at[a, tile])

    def forward(tile, stats, start, size):
        top, total, dots = stats
        keys = rows_at(start, size)
        scores = mm(kb[keys, :], qt[...], 1, 0)
        dprobs = mm(vb[keys, :], gt[...], 1, 0)
        top_new = jnp.maximum(top, jnp.ceil(jnp.max(scores, axis=0, keepdims=True) * SCALE2))
        e = jnp.exp2(scores * SCALE2 - top_new)
        shrink = jnp.exp2(top - top_new)
        total = total * shrink + jnp.sum(e, axis=0, keepdims=True)
        dots = dots * shrink + jnp.sum(e * dprobs, axis=0, keepdims=True)
        e_s[keys, :] = e.astype(BF16)
        dp_s[keys, :] = dprobs
        m_s[pl.ds(tile, 1), :] = top_new
        return top_new, total, dots

    def end_forward(stats):
        top, total, dots = stats
        inverse = 1.0 / total
        gi[...] = (gt[...].astype(F32) * inverse).astype(BF16)
        qi[...] = (qt[...].astype(F32) * (inverse * SCALE)).astype(BF16)
        return top, dots * inverse, inverse * SCALE

    def backward(tile, stats, start, size, first=False, pair=False):
        top, mean, _ = stats
        keys = rows_at(start, size)
        last = m_s[pl.ds(tile, 1), :]
        e = e_s[keys, :]
        if pair:
            step = jnp.exp2(m_s[pl.ds(tile - 1, 1), :] - last).astype(BF16)
            e = jnp.concatenate([e[: size // 2] * step, e[size // 2 :]], 0)
        factor = jnp.exp2(last - top)
        low = factor.astype(BF16)
        ds = (e.astype(F32) * (dp_s[keys, :] - mean)).astype(BF16)
        part_v = mm(e, gi[...] * low, 1, 1)
        va[keys, :] = part_v if first else va[keys, :] + part_v
        part_k = mm(ds, qi[...] * low, 1, 1)
        ka[keys, :] = part_k if first else ka[keys, :] + part_k
        dqa[...] += mm(kb[keys, :], ds, 0, 0) * factor

    def out_copy(a, src, dst, slot):
        device, _ = chip(slot, -1)
        return pltpu.make_async_remote_copy(
            src_ref=src,
            dst_ref=dst.at[0, :, feat(head)],
            send_sem=out_s.at[a],
            recv_sem=out_r.at[a],
            device_id=device,
            device_id_type=MESH,
        )

    def send_out(a, src, dst, slot):
        @pl.when(slot > 0)
        def _():
            out_copy(a, src, dst, slot).start()

        @pl.when(slot == 0)
        def _():
            pltpu.make_async_copy(src, dst.at[0, :, feat(head)], out_r.at[a]).start()

    def send_dq(half, stats):
        dqb[pl.ds(half * QB, QB), :] = (dqa[...] * stats[2]).T.astype(BF16)

        def one(slot, carry):
            send_out(0, dqb.at[rows_at(slot * ROWS, ROWS)], dq_o, slot)
            return carry

        lax.fori_loop(half * HALF_SLOTS, (half + 1) * HALF_SLOTS, one, 0)

    low = jnp.full((1, QB), -1e30, F32)
    zero = jnp.zeros((1, QB), F32)
    start = (low, zero, zero)

    def step_first(tile, stats):
        @pl.when(tile < TILES - 1)
        def _():
            pass_keys(tile + 1)

        @pl.when(tile == TILES - 2)
        def _():
            lax.fori_loop(HALF_SLOTS, SLOTS, send_q, 0)

        take_keys(tile)
        with jax.named_scope("forward_first"):
            return forward(tile, stats, tile * KT, KT)

    lax.fori_loop(4, 8, send_k, 0)
    take_queries(0)
    lax.fori_loop(8, 12, send_k, 0)
    stats = forward(TILES, start, KEYS, COND)
    pass_keys(0)
    lax.fori_loop(12, SLOTS, send_k, 0)
    stats = end_forward(lax.fori_loop(0, TILES, step_first, stats))

    def back_first(tile, carry):
        backward(2 * tile + 1, stats, tile * BT, BT, True, True)
        return carry

    backward(TILES, stats, KEYS, COND, True)
    with jax.named_scope("backward_first"):
        lax.fori_loop(0, BACK_TILES, back_first, 0)
    with jax.named_scope("send_dq"):
        send_dq(0, stats)

    def step_second(tile, stats):
        with jax.named_scope("forward_second"):
            return forward(tile, stats, tile * BT, BT)

    take_queries(1)
    stats = forward(TILES, start, KEYS, COND)
    stats = end_forward(lax.fori_loop(0, BACK_TILES, step_second, stats))

    backward(TILES, stats, KEYS, COND)

    @pl.when(core == 0)
    def _():
        c_st[...] = va[pl.ds(KEYS, COND), :].astype(BF16)

    @pl.when(core == 1)
    def _():
        c_st[...] = ka[pl.ds(KEYS, COND), :].astype(BF16)

    pltpu.make_async_remote_copy(
        src_ref=c_st, dst_ref=c_rx, send_sem=c1_s, recv_sem=c1_r, device_id=partner, device_id_type=MESH
    ).start()

    def cond_sum():
        arrived(c_rx, c1_r)

        @pl.when(core == 0)
        def _():
            cga[0] = (ka[pl.ds(KEYS, COND), :] + c_rx[...].astype(F32)).astype(BF16)

        @pl.when(core == 1)
        def _():
            cga[0] = (va[pl.ds(KEYS, COND), :] + c_rx[...].astype(F32)).astype(BF16)

        for dz in range(1, 8):
            pltpu.make_async_remote_copy(
                src_ref=cga.at[0],
                dst_ref=cga.at[dz],
                send_sem=cg_s,
                recv_sem=cg_r,
                device_id={"dp": (z + dz) % 8},
                device_id_type=MESH,
            ).start()

    def part_copy(dt):
        owner = (tp + dt) % 4
        return pltpu.make_async_remote_copy(
            src_ref=prod.at[pl.ds(pl.multiple_of((z % 2) * 64 + owner * 112, 16), 112)],
            dst_ref=w_o.at[tp],
            send_sem=w_s,
            recv_sem=w_r,
            device_id={"tp": owner},
            device_id_type=MESH,
        )

    def cond_product():
        arrived(hida.at[pl.ds(1, 7)], hid_r)
        arrived(cga.at[pl.ds(1, 7)], cg_r)
        prod[...] = mm(
            hida[...].reshape(8 * COND, WINDOW), cga[...].reshape(8 * COND, HD), 0, 0
        )
        for dt in range(1, 4):
            part_copy(dt).start()
        pltpu.make_async_copy(
            prod.at[pl.ds(pl.multiple_of((z % 2) * 64 + tp * 112, 16), 112)], w_o.at[tp], w_r
        ).start()

    def tile_slots(tile):
        return pl.ds(pl.multiple_of(tile * BACK_SLOTS, BACK_SLOTS), BACK_SLOTS)

    def swap(tile):
        for i in range(BACK_SLOTS):
            slot = tile * BACK_SLOTS + i
            theirs = rows_at(slot * 2 * ROWS + (1 - core) * ROWS, ROWS)
            st[0, slot] = ka[theirs, :].astype(BF16)
            st[1, slot] = va[theirs, :].astype(BF16)
        for a in range(2):
            pltpu.make_async_remote_copy(
                src_ref=st.at[a, tile_slots(tile)],
                dst_ref=rx.at[a, tile_slots(tile)],
                send_sem=ex_s.at[a],
                recv_sem=ex_r.at[a, tile],
                device_id=partner,
                device_id_type=MESH,
            ).start()

    def finish(tile):
        for a in range(2):
            arrived(rx.at[a, tile_slots(tile)], ex_r.at[a, tile])
        for i in range(BACK_SLOTS):
            slot = tile * BACK_SLOTS + i
            mine = rows_at(slot * 2 * ROWS + core * ROWS, ROWS)
            for a, (acc, dst) in enumerate(((ka, dk_o), (va, dv_o))):
                fin[a, slot] = (acc[mine, :] + rx[a, slot].astype(F32)).astype(BF16)
                send_out(1 + a, fin.at[a, slot], dst, slot)

    def back(tile, carry):
        with jax.named_scope("backward_tile"):
            backward(tile, stats, tile * BT, BT)
        swap(tile)

        @pl.when(tile > 0)
        def _():
            with jax.named_scope("finish"):
                finish(tile - 1)

        @pl.when(tile == 1)
        def _():
            with jax.named_scope("condition_sum"):
                cond_sum()

        return carry

    lax.fori_loop(0, BACK_TILES, back, 0)
    with jax.named_scope("send_dq"):
        send_dq(1, stats)
    with jax.named_scope("finish"):
        finish(BACK_TILES - 1)
    with jax.named_scope("condition_product"):
        cond_product()

    with jax.named_scope("drain"):
        sent = pl.ds(0, (SLOTS - 1) * ROWS)
        for a in range(4):
            arrived(qb.at[sent], in_s.at[a])
        for a in range(2):
            arrived(qb, fw_s.at[a])
            arrived(st.at[a], ex_s.at[a])
        arrived(c_st, c1_s)
        arrived(hida.at[pl.ds(1, 7)], hid_s)
        arrived(cga.at[pl.ds(1, 7)], cg_s)
        for a in range(3):
            arrived(dqb.at[sent], out_s.at[a])
        arrived(w_o.at[pl.ds(0, 3)], w_s)
        arrived(w_o, w_r)
        for a, dst in enumerate((dq_o, dk_o, dv_o)):
            arrived(dst.at[0], out_r.at[a])


def place(dq, dk, dv, parts, dq_o, dk_o, dv_o, w_o, held, held_w, in_s, out_s, w_s):
    fetch_w = pltpu.make_async_copy(parts, held_w, w_s)
    fetches = [
        pltpu.make_async_copy(src, held.at[a], in_s.at[a]) for a, src in enumerate((dq, dk, dv))
    ]
    stores = [
        pltpu.make_async_copy(held.at[a], dst, out_s.at[a])
        for a, dst in enumerate((dq_o, dk_o, dv_o))
    ]
    for fetch in fetches:
        fetch.start()
    fetch_w.start()
    for fetch, store in zip(fetches, stores):
        fetch.wait()
        store.start()
    fetch_w.wait()
    for half in range(2):
        for array in range(2):
            w_o[:, array, half * HD : (half + 1) * HD] = held_w[2 * half + array]
    for store in stores:
        store.wait()


def on_device(latent_query, latent_key, latent_value, out_grad, query_hidden, cond_weight):
    anywhere = pl.BlockSpec(memory_space=pl.ANY)
    token = jax.ShapeDtypeStruct(latent_query.shape, BF16)
    dma = pltpu.SemaphoreType.DMA
    total_keys = KEYS + COND
    grads = pl.pallas_call(
        kernel,
        name="attention_backward",
        out_shape=(token, token, token, jax.ShapeDtypeStruct((4, 112, HD), F32)),
        in_specs=[anywhere] * 4 + [pl.BlockSpec(memory_space=pltpu.VMEM), anywhere],
        out_specs=(anywhere,) * 4,
        scratch_shapes=[
            pltpu.VMEM((2 * QB, HD), BF16),
            pltpu.VMEM((2 * QB, HD), BF16),
            pltpu.VMEM((total_keys, HD), BF16),
            pltpu.VMEM((total_keys, HD), BF16),
            pltpu.VMEM((HD, QB), BF16),
            pltpu.VMEM((HD, QB), BF16),
            pltpu.VMEM((HD, QB), BF16),
            pltpu.VMEM((HD, QB), BF16),
            pltpu.VMEM((total_keys, QB), BF16),
            pltpu.VMEM((total_keys, QB), F32),
            pltpu.VMEM((16, QB), F32),
            pltpu.VMEM((total_keys, HD), F32),
            pltpu.VMEM((total_keys, HD), F32),
            pltpu.VMEM((HD, QB), F32),
            pltpu.VMEM((2 * QB, HD), BF16),
            pltpu.VMEM((2, SLOTS, ROWS, HD), BF16),
            pltpu.VMEM((2, SLOTS, ROWS, HD), BF16),
            pltpu.VMEM((2, SLOTS, ROWS, HD), BF16),
            pltpu.VMEM((cond_weight.shape[0], 2, HD), BF16),
            pltpu.VMEM((8, COND, WINDOW), BF16),
            pltpu.VMEM((COND, HD), BF16),
            pltpu.VMEM((COND, HD), BF16),
            pltpu.VMEM((8, COND, HD), BF16),
            pltpu.VMEM((WINDOW, HD), F32),
            dma((4,)), dma((2, SLOTS // GROUP)), dma((2, TILES)),
            dma((2,)), dma((2, TILES)),
            dma((2,)), dma((2, BACK_TILES)),
            dma((3,)), dma((3,)),
            dma, dma,
            dma, dma,
            dma, dma,
            dma, dma,
            dma,
        ],
        compiler_params=pltpu.CompilerParams(
            collective_id=0, has_side_effects=True, vmem_limit_bytes=60 << 20
        ),
    )(latent_query, latent_key, latent_value, out_grad, query_hidden, cond_weight)
    weight = jax.ShapeDtypeStruct((112, 2, 2 * HD), F32)
    return pl.pallas_call(
        place,
        name="place_outputs",
        out_shape=(token, token, token, weight),
        in_specs=[anywhere] * 4,
        out_specs=(anywhere,) * 3 + (pl.BlockSpec(memory_space=pltpu.VMEM),),
        scratch_shapes=[
            pltpu.VMEM((3,) + latent_query.shape, BF16),
            pltpu.VMEM((4, 112, HD), F32),
            dma((3,)), dma((3,)), dma,
        ],
    )(*grads)


def solution(mesh):
    placed = (
        P("dp", ("seq", "tp"), None),
        P("dp", ("seq", "tp"), None),
        P("dp", ("seq", "tp"), None),
        P("dp", ("seq", "tp"), None),
        P("dp", None, None),
        P(None, None, "seq"),
    )
    return jax.shard_map(
        on_device,
        mesh=mesh,
        in_specs=placed,
        out_specs=(
            P("dp", ("seq", "tp"), None),
            P("dp", ("seq", "tp"), None),
            P("dp", ("seq", "tp"), None),
            P(("dp", "tp"), None, "seq"),
        ),
        check_vma=False,
    )
```

time: 98.7 us -> 76.9 us (0.78)
  Pallas kernels: 90.1 us -> 76.1 us
  local copies, waits for them, and re-layouts: 7.71 us -> 0 us
    pallas_call x1, Pallas kernels: 90.1 us -> 73.2 us  [on_device(): pl.pallas_call(kernel, name='attention_backward', out_shape=(token, token...]
    unnamed x3 -> x0, local copies, waits for them, and re-layouts: 5.64 us -> none
    pallas_call x0 -> x1, Pallas kernels: none -> 2.93 us  [on_device(): pl.pallas_call(place, name='place_outputs', out_shape=(token, token, toke...]
    transpose x1 -> x0, local copies, waits for them, and re-layouts: 1.12 us -> none  [on_device(): parts.reshape(2, 2, 112, HD).transpose(2, 1, 0, 3).reshape(112, 2, 2 * HD)]
where the time goes in v2:
time: 76.9 us; the launch traced here: 76.8 us
  Pallas kernels  76.1 us (99%)
    pallas_call x1, Pallas kernels, on_device(): pl.pallas_call(kernel, name='attention_backward', out_shape=(token, token...  73.2 us
    pallas_call x1, Pallas kernels, on_device(): pl.pallas_call(place, name='place_outputs', out_shape=(token, token, toke...  2.93 us

profile of v2, /device:TPU:1, one launch (start us, length us, event | category | flops | bytes accessed | tf_op | source)
XLA Modules:
  0.0 76.8 jit_solution(5576286883761838526)
XLA Ops:
  0.6 73.2 %attention_backward.1 = (bf16[1,128,2048]{2,1,0:T(8,128)(2,1)}, bf16[1,128,2048]{2,1,0:T(8,128)(2,1)}, bf16[1,128,2048]{2,1,0:T(8,128)(2,1)}, f32[4,112,128]{2,1,0:T(8,128)}) custom-call(bf16[1,128,2048]{2,1,0:T(8,128)(2,1)} %lq.1, bf16[1,128,2048]{2,1,0:T(8,128)(2,1)} %lk.1, bf16[1,128,2048]{2,1,0:T(8,128)(2,1)} %lv.1, bf16[1,128,2048]{2,1,0:T(8,128)(2,1)} %og.1, ...), custom_call_target="tpu_custom_call" | custom-call | tf_op jit(solution)/shard_map/attention_backward/pallas_call | solution.py:460
  73.8 2.9 %place_outputs.1 = (bf16[1,128,2048]{2,1,0:T(8,128)(2,1)}, bf16[1,128,2048]{2,1,0:T(8,128)(2,1)}, bf16[1,128,2048]{2,1,0:T(8,128)(2,1)}, f32[112,2,256]{2,1,0:T(2,128)}) custom-call(bf16[1,128,2048]{2,1,0:T(8,128)(2,1)} %get-tuple-element.8.dq, bf16[1,128,2048]{2,1,0:T(8,128)(2,1)} %get-tuple-element.9.dk, bf16[1,128,2048]{2,1,0:T(8,128)(2,1)} %get-tuple-element.10.dv, ...), custom_call_target="tpu_custom_call" | custom-call | tf_op jit(solution)/shard_map/place_outputs/pallas_call | solution.py:506

commit v3 on v2

v3 whole, which is shorter than its diff:
```python
import jax
import jax.numpy as jnp
from jax import lax
from jax.experimental import pallas as pl
from jax.experimental.pallas import tpu as pltpu
from jax.sharding import PartitionSpec as P

HD = 128
MESH = pl.DeviceIdType.MESH
F32 = jnp.float32
BF16 = jnp.bfloat16
SCALE = HD ** (-0.5)
SCALE2 = SCALE * 1.4426950408889634
ROWS = 128
SLOTS = 16
QB = 1024
KT = 512
BT = 2 * KT
KEYS = 4096
COND = 64
TILES = KEYS // KT
TILE_SLOTS = SLOTS // TILES
BACK_TILES = KEYS // BT
BACK_SLOTS = SLOTS // BACK_TILES
HALF_SLOTS = QB // ROWS
GROUP = 4
WINDOW = 512


def mm(a, b, ca, cb):
    return lax.dot_general(a, b, (((ca,), (cb,)), ((), ())), preferred_element_type=F32)


OFFSETS = (
    (0, 0), (0, 1), (1, 0), (0, 3), (3, 0), (1, 1), (3, 3), (2, 0),
    (0, 2), (1, 3), (3, 1), (1, 2), (2, 1), (3, 2), (2, 3), (2, 2),
)


def pick(slot, values):
    if isinstance(slot, int):
        return values[slot]
    out = values[0]
    for k in range(1, len(values)):
        if values[k] != values[k - 1]:
            out = jnp.where(slot >= k, values[k], out)
    return out


def offset_of(slot):
    return pick(slot, [dx for dx, _ in OFFSETS]), pick(slot, [dy for _, dy in OFFSETS])


def rows_at(start, size):
    if isinstance(start, int):
        return pl.ds(start, size)
    return pl.ds(pl.multiple_of(start, 64), size)


def arrived(ref, sem):
    pltpu.make_async_copy(ref, ref, sem).wait()


def kernel(
    lq, lk, lv, og, hidden, cw,
    dq_o, dk_o, dv_o, w_o,
    qb, gb, kb, vb, qt, gt, qi, gi, e_s, dp_s, m_s, ka, va, dqa, dqb,
    st, rx, fin, cwv, hid, hida, c_st, c_rx, cga, prod,
    in_s, q_r, k_r, fw_s, fw_r, ex_s, ex_r, out_s, out_r,
    hid_s, hid_r, c1_s, c1_r, cg_s, cg_r, w_s, w_r, cw_sem, hid_sem,
):
    z = lax.axis_index("dp")
    seq = lax.axis_index("seq")
    tp = lax.axis_index("tp")
    x = (seq // 4) * 2 + tp // 2
    y = seq % 4
    core = tp % 2
    head = 2 * seq + tp // 2
    partner = {"tp": (tp // 2) * 2 + 1 - core}

    def chip(slot, sign):
        dx, dy = offset_of(slot)
        cx = (x + sign * dx + 4) % 4
        cy = (y + sign * dy + 4) % 4
        cseq = (cx // 2) * 4 + cy
        return {"seq": cseq, "tp": (cx % 2) * 2 + core}, 2 * cseq + cx % 2

    def feat(index):
        return pl.ds(pl.multiple_of(index * HD, HD), HD)

    barrier = pltpu.get_barrier_semaphore()

    for slot in range(1, SLOTS):
        device, _ = chip(slot, 1)
        pl.semaphore_signal(barrier, inc=1, device_id=device, device_id_type=MESH)
    pl.semaphore_signal(barrier, inc=1, device_id=partner, device_id_type=MESH)
    pl.semaphore_signal(barrier, inc=1, device_id={"tp": 3 - tp}, device_id_type=MESH)
    for dz in range(1, 8):
        pl.semaphore_signal(
            barrier, inc=1, device_id={"dp": (z + dz) % 8}, device_id_type=MESH
        )

    weights = pltpu.make_async_copy(
        cw.at[:, :, feat(tp // 2)], cwv, cw_sem
    )
    weights.start()
    rows = pltpu.make_async_copy(hidden, hid, hid_sem)
    rows.start()
    for a, (src, dst) in enumerate(((lq, qb), (og, gb))):
        pltpu.make_async_copy(src.at[0, :, feat(head)], dst.at[pl.ds(0, ROWS)], q_r.at[a, 0]).start()
    for a, (src, dst) in enumerate(((lk, kb), (lv, vb))):
        pltpu.make_async_copy(
            src.at[0, :, feat(head)], dst.at[rows_at(core * ROWS, ROWS)], k_r.at[a, 0]
        ).start()

    with jax.named_scope("barrier"):
        pl.semaphore_wait(barrier, 24)

    def in_copy(a, src, dst, dst_start, slot, arrival):
        device, there = chip(slot, 1)
        return pltpu.make_async_remote_copy(
            src_ref=src.at[0, :, feat(there)],
            dst_ref=dst.at[rows_at(dst_start, ROWS)],
            send_sem=in_s.at[a],
            recv_sem=arrival,
            device_id=device,
            device_id_type=MESH,
        )

    def send_q(slots):
        for slot in slots:
            for a, (src, dst) in enumerate(((lq, qb), (og, gb))):
                in_copy(a, src, dst, slot * ROWS, slot, q_r.at[a, slot // GROUP]).start()

    def send_k(slots):
        for slot in slots:
            row = slot * 2 * ROWS + core * ROWS
            for a, (src, dst) in enumerate(((lk, kb), (lv, vb))):
                in_copy(2 + a, src, dst, row, slot, k_r.at[a, slot // TILE_SLOTS]).start()

    with jax.named_scope("send_inputs"):
        send_q(range(1, HALF_SLOTS))
        send_k(range(1, SLOTS))

    def window(zz):
        return pl.ds(pl.multiple_of((7 * zz // 2) * HD, HD), WINDOW)

    rows.wait()
    for dz in range(1, 8):
        there = (z + dz) % 8
        pltpu.make_async_remote_copy(
            src_ref=hid.at[0, :, window(there)],
            dst_ref=hida.at[dz],
            send_sem=hid_s,
            recv_sem=hid_r,
            device_id={"dp": there},
            device_id_type=MESH,
        ).start()
    hida[0] = hid[0, :, window(z)]
    weights.wait()

    def cond_step(i, sums):
        r = pl.multiple_of(i * 512, 512)
        rows = hid[0, :, pl.ds(r, 512)]
        return (
            sums[0] + mm(rows, cwv[pl.ds(r, 512), 0, :], 1, 0),
            sums[1] + mm(rows, cwv[pl.ds(r, 512), 1, :], 1, 0),
        )

    nothing = jnp.zeros((COND, HD), F32)
    with jax.named_scope("condition_keys"):
        cond_k, cond_v = lax.fori_loop(0, 7, cond_step, (nothing, nothing))
    kb[pl.ds(KEYS, COND), :] = cond_k.astype(BF16)
    vb[pl.ds(KEYS, COND), :] = cond_v.astype(BF16)

    def take_queries(half):
        for group in (2 * half, 2 * half + 1):
            with jax.named_scope("wait_queries"):
                for a, dst in enumerate((qb, gb)):
                    arrived(dst.at[pl.ds(group * GROUP * ROWS, GROUP * ROWS)], q_r.at[a, group])
        qt[half] = qb[pl.ds(half * QB, QB), :].T
        gt[half] = gb[pl.ds(half * QB, QB), :].T
        dqa[half] = jnp.zeros((HD, QB), F32)

    def pass_keys(tile):
        with jax.named_scope("wait_keys"):
            for a, dst in enumerate((kb, vb)):
                arrived(dst.at[pl.ds(0, TILE_SLOTS * ROWS)], k_r.at[a, tile])
        for i in range(TILE_SLOTS):
            for a, dst in enumerate((kb, vb)):
                mine = dst.at[rows_at((tile * TILE_SLOTS + i) * 2 * ROWS + core * ROWS, ROWS)]
                pltpu.make_async_remote_copy(
                    src_ref=mine,
                    dst_ref=mine,
                    send_sem=fw_s.at[a],
                    recv_sem=fw_r.at[a, tile],
                    device_id=partner,
                    device_id_type=MESH,
                ).start()

    def take_keys(tile):
        with jax.named_scope("wait_partner_keys"):
            for a, dst in enumerate((kb, vb)):
                arrived(dst.at[pl.ds(0, TILE_SLOTS * ROWS)], fw_r.at[a, tile])

    def forward(half, tile, stats, start, size):
        top, total, dots = stats
        keys = rows_at(start, size)
        scores = mm(kb[keys, :], qt[half], 1, 0)
        dprobs = mm(vb[keys, :], gt[half], 1, 0)
        top_new = jnp.maximum(top, jnp.ceil(jnp.max(scores, axis=0, keepdims=True) * SCALE2))
        e = jnp.exp2(scores * SCALE2 - top_new)
        shrink = jnp.exp2(top - top_new)
        total = total * shrink + jnp.sum(e, axis=0, keepdims=True)
        dots = dots * shrink + jnp.sum(e * dprobs, axis=0, keepdims=True)
        e_s[half, keys, :] = e.astype(BF16)
        if half == 0:
            dp_s[keys, :] = dprobs
        m_s[half, pl.ds(tile, 1), :] = top_new
        return top_new, total, dots

    def end_forward(half, stats):
        top, total, dots = stats
        inverse = 1.0 / total
        gi[half] = (gt[half].astype(F32) * inverse).astype(BF16)
        qi[half] = (qt[half].astype(F32) * (inverse * SCALE)).astype(BF16)
        return top, dots * inverse, inverse * SCALE

    def backward(half, tile, stats, start, size, first=False, pair=False):
        top, mean, _ = stats
        keys = rows_at(start, size)
        last = m_s[half, pl.ds(tile, 1), :]
        e = e_s[half, keys, :]
        if pair:
            step = jnp.exp2(m_s[half, pl.ds(tile - 1, 1), :] - last).astype(BF16)
            e = jnp.concatenate([e[: size // 2] * step, e[size // 2 :]], 0)
        factor = jnp.exp2(last - top)
        low = factor.astype(BF16)
        part_v = mm(e, gi[half] * low, 1, 1)
        va[keys, :] = part_v if first else va[keys, :] + part_v
        dprobs = dp_s[keys, :] if half == 0 else mm(vb[keys, :], gt[half], 1, 0)
        ds = (e.astype(F32) * (dprobs - mean)).astype(BF16)
        part_k = mm(ds, qi[half] * low, 1, 1)
        ka[keys, :] = part_k if first else ka[keys, :] + part_k
        dqa[half] += mm(kb[keys, :], ds, 0, 0) * factor

    def out_copy(a, src, dst, slot):
        device, _ = chip(slot, -1)
        return pltpu.make_async_remote_copy(
            src_ref=src,
            dst_ref=dst.at[0, :, feat(head)],
            send_sem=out_s.at[a],
            recv_sem=out_r.at[a],
            device_id=device,
            device_id_type=MESH,
        )

    def send_out(a, src, dst, slot):
        def here():
            pltpu.make_async_copy(src, dst.at[0, :, feat(head)], out_r.at[a]).start()

        def there():
            out_copy(a, src, dst, slot).start()

        if isinstance(slot, int):
            there() if slot else here()
        else:
            pl.when(slot > 0)(there)
            pl.when(slot == 0)(here)

    def send_dq(half, stats):
        with jax.named_scope("send_dq"):
            dqb[pl.ds(half * QB, QB), :] = (dqa[half] * stats[2]).T.astype(BF16)
            for slot in range(half * HALF_SLOTS, (half + 1) * HALF_SLOTS):
                send_out(0, dqb.at[pl.ds(slot * ROWS, ROWS)], dq_o, slot)

    low = jnp.full((1, QB), -1e30, F32)
    zero = jnp.zeros((1, QB), F32)
    start = (low, zero, zero)

    def step_first(tile, stats):
        @pl.when(tile < TILES - 1)
        def _():
            pass_keys(tile + 1)

        @pl.when(tile == 3)
        def _():
            send_q(range(HALF_SLOTS, SLOTS))

        take_keys(tile)
        with jax.named_scope("forward_first"):
            return forward(0, tile, stats, tile * KT, KT)

    take_queries(0)
    first = forward(0, TILES, start, KEYS, COND)
    pass_keys(0)
    first = end_forward(0, lax.fori_loop(0, TILES, step_first, first))

    last = BACK_TILES - 1
    with jax.named_scope("backward_first"):
        backward(0, TILES, first, KEYS, COND, True)
        for tile in (last, last - 1):
            backward(0, 2 * tile + 1, first, tile * BT, BT, True, True)

    def step_second(tile, stats):
        with jax.named_scope("forward_second"):
            return forward(1, tile, stats, tile * BT, BT)

    take_queries(1)
    second = forward(1, BACK_TILES, start, KEYS, COND)
    second = end_forward(1, lax.fori_loop(0, BACK_TILES, step_second, second))
    backward(1, BACK_TILES, second, KEYS, COND)

    @pl.when(core == 0)
    def _():
        c_st[...] = va[pl.ds(KEYS, COND), :].astype(BF16)

    @pl.when(core == 1)
    def _():
        c_st[...] = ka[pl.ds(KEYS, COND), :].astype(BF16)

    pltpu.make_async_remote_copy(
        src_ref=c_st, dst_ref=c_rx, send_sem=c1_s, recv_sem=c1_r, device_id=partner, device_id_type=MESH
    ).start()

    def cond_sum():
        arrived(c_rx, c1_r)

        @pl.when(core == 0)
        def _():
            cga[0] = (ka[pl.ds(KEYS, COND), :] + c_rx[...].astype(F32)).astype(BF16)

        @pl.when(core == 1)
        def _():
            cga[0] = (va[pl.ds(KEYS, COND), :] + c_rx[...].astype(F32)).astype(BF16)

        for dz in range(1, 8):
            pltpu.make_async_remote_copy(
                src_ref=cga.at[0],
                dst_ref=cga.at[dz],
                send_sem=cg_s,
                recv_sem=cg_r,
                device_id={"dp": (z + dz) % 8},
                device_id_type=MESH,
            ).start()

    def part_copy(dt):
        owner = (tp + dt) % 4
        return pltpu.make_async_remote_copy(
            src_ref=prod.at[pl.ds(pl.multiple_of((z % 2) * 64 + owner * 112, 16), 112)],
            dst_ref=w_o.at[tp],
            send_sem=w_s,
            recv_sem=w_r,
            device_id={"tp": owner},
            device_id_type=MESH,
        )

    def cond_product():
        arrived(hida.at[pl.ds(1, 7)], hid_r)
        arrived(cga.at[pl.ds(1, 7)], cg_r)
        prod[...] = mm(
            hida[...].reshape(8 * COND, WINDOW), cga[...].reshape(8 * COND, HD), 0, 0
        ).astype(BF16)
        for dt in range(1, 4):
            part_copy(dt).start()
        pltpu.make_async_copy(
            prod.at[pl.ds(pl.multiple_of((z % 2) * 64 + tp * 112, 16), 112)], w_o.at[tp], w_r
        ).start()

    def swap(unit, slot, count):
        for i in range(count):
            theirs = rows_at((slot + i) * 2 * ROWS + (1 - core) * ROWS, ROWS)
            st[0, slot + i] = ka[theirs, :].astype(BF16)
            st[1, slot + i] = va[theirs, :].astype(BF16)
        for a in range(2):
            part = pl.ds(slot, count)
            pltpu.make_async_remote_copy(
                src_ref=st.at[a, part],
                dst_ref=rx.at[a, part],
                send_sem=ex_s.at[a],
                recv_sem=ex_r.at[a, unit],
                device_id=partner,
                device_id_type=MESH,
            ).start()

    def finish(unit, slot, count):
        with jax.named_scope("finish"):
            for a in range(2):
                arrived(rx.at[a, pl.ds(slot, count)], ex_r.at[a, unit])
            for i in range(count):
                mine = rows_at((slot + i) * 2 * ROWS + core * ROWS, ROWS)
                for a, (acc, dst) in enumerate(((ka, dk_o), (va, dv_o))):
                    fin[a, slot + i] = (acc[mine, :] + rx[a, slot + i].astype(F32)).astype(BF16)
                    send_out(1 + a, fin.at[a, slot + i], dst, slot + i)

    for unit in range(2):
        with jax.named_scope("backward_tile"):
            backward(1, last, second, last * BT + unit * KT, KT)
        swap(unit, last * BACK_SLOTS + unit * 2, 2)
    with jax.named_scope("condition_sum"):
        cond_sum()
    finish(0, last * BACK_SLOTS, 2)

    with jax.named_scope("backward_tile"):
        backward(1, last - 1, second, (last - 1) * BT, BT)
    swap(2, (last - 1) * BACK_SLOTS, BACK_SLOTS)
    finish(1, last * BACK_SLOTS + 2, 2)

    def back(step, carry):
        tile = last - step
        with jax.named_scope("backward_tile"):
            backward(1, tile, second, tile * BT, BT, True)

        @pl.when(tile == 0)
        def _():
            send_dq(1, second)

        @pl.when(step == 2)
        def _():
            with jax.named_scope("condition_product"):
                cond_product()

        finish(step, (tile + 1) * BACK_SLOTS, BACK_SLOTS)
        with jax.named_scope("backward_tile"):
            backward(0, 2 * tile + 1, first, tile * BT, BT, False, True)
        swap(step + 1, tile * BACK_SLOTS, BACK_SLOTS)
        return carry

    lax.fori_loop(2, BACK_TILES, back, 0)
    send_dq(0, first)
    finish(BACK_TILES, 0, BACK_SLOTS)

    with jax.named_scope("drain"):
        sent = pl.ds(0, (SLOTS - 1) * ROWS)
        for a in range(4):
            arrived(qb.at[sent], in_s.at[a])
        for a in range(2):
            arrived(qb, fw_s.at[a])
            arrived(st.at[a], ex_s.at[a])
        arrived(c_st, c1_s)
        arrived(hida.at[pl.ds(1, 7)], hid_s)
        arrived(cga.at[pl.ds(1, 7)], cg_s)
        for a in range(3):
            arrived(dqb.at[sent], out_s.at[a])
    with jax.named_scope("drain_weight"):
        arrived(w_o.at[pl.ds(0, 3)], w_s)
        arrived(w_o, w_r)
    with jax.named_scope("drain_key"):
        arrived(dk_o.at[0], out_r.at[1])
    with jax.named_scope("drain_value"):
        arrived(dv_o.at[0], out_r.at[2])
    with jax.named_scope("drain_query"):
        arrived(dq_o.at[0], out_r.at[0])


def place(dq, dk, dv, parts, dq_o, dk_o, dv_o, w_o, held, held_w, full_w, in_s, out_s, w_s):
    fetch_w = pltpu.make_async_copy(parts, held_w, w_s.at[0])
    store_w = pltpu.make_async_copy(full_w, w_o, w_s.at[1])
    fetches = [
        pltpu.make_async_copy(src, held.at[a], in_s.at[a]) for a, src in enumerate((dq, dk, dv))
    ]
    stores = [
        pltpu.make_async_copy(held.at[a], dst, out_s.at[a])
        for a, dst in enumerate((dq_o, dk_o, dv_o))
    ]
    fetch_w.start()
    for fetch in fetches:
        fetch.start()
    fetch_w.wait()
    for half in range(2):
        for array in range(2):
            columns = slice(half * HD, (half + 1) * HD)
            full_w[:, array, columns] = held_w[2 * half + array].astype(F32)
    store_w.start()
    for fetch, store in zip(fetches, stores):
        fetch.wait()
        store.start()
    store_w.wait()
    for store in stores:
        store.wait()


def on_device(latent_query, latent_key, latent_value, out_grad, query_hidden, cond_weight):
    anywhere = pl.BlockSpec(memory_space=pl.ANY)
    token = jax.ShapeDtypeStruct(latent_query.shape, BF16)
    dma = pltpu.SemaphoreType.DMA
    total_keys = KEYS + COND
    grads = pl.pallas_call(
        kernel,
        name="attention_backward",
        out_shape=(token, token, token, jax.ShapeDtypeStruct((4, 112, HD), BF16)),
        in_specs=[anywhere] * 6,
        out_specs=(anywhere,) * 4,
        scratch_shapes=[
            pltpu.VMEM((2 * QB, HD), BF16),
            pltpu.VMEM((2 * QB, HD), BF16),
            pltpu.VMEM((total_keys, HD), BF16),
            pltpu.VMEM((total_keys, HD), BF16),
            pltpu.VMEM((2, HD, QB), BF16),
            pltpu.VMEM((2, HD, QB), BF16),
            pltpu.VMEM((2, HD, QB), BF16),
            pltpu.VMEM((2, HD, QB), BF16),
            pltpu.VMEM((2, total_keys, QB), BF16),
            pltpu.VMEM((total_keys, QB), F32),
            pltpu.VMEM((2, 16, QB), F32),
            pltpu.VMEM((total_keys, HD), F32),
            pltpu.VMEM((total_keys, HD), F32),
            pltpu.VMEM((2, HD, QB), F32),
            pltpu.VMEM((2 * QB, HD), BF16),
            pltpu.VMEM((2, SLOTS, ROWS, HD), BF16),
            pltpu.VMEM((2, SLOTS, ROWS, HD), BF16),
            pltpu.VMEM((2, SLOTS, ROWS, HD), BF16),
            pltpu.VMEM((cond_weight.shape[0], 2, HD), BF16),
            pltpu.VMEM(query_hidden.shape, BF16),
            pltpu.VMEM((8, COND, WINDOW), BF16),
            pltpu.VMEM((COND, HD), BF16),
            pltpu.VMEM((COND, HD), BF16),
            pltpu.VMEM((8, COND, HD), BF16),
            pltpu.VMEM((WINDOW, HD), BF16),
            dma((4,)), dma((2, SLOTS // GROUP)), dma((2, TILES)),
            dma((2,)), dma((2, TILES)),
            dma((2,)), dma((2, BACK_TILES + 1)),
            dma((3,)), dma((3,)),
            dma, dma,
            dma, dma,
            dma, dma,
            dma, dma,
            dma, dma,
        ],
        compiler_params=pltpu.CompilerParams(
            collective_id=0, has_side_effects=True, vmem_limit_bytes=60 << 20
        ),
    )(latent_query, latent_key, latent_value, out_grad, query_hidden, cond_weight)
    weight = jax.ShapeDtypeStruct((112, 2, 2 * HD), F32)
    return pl.pallas_call(
        place,
        name="place_outputs",
        out_shape=(token, token, token, weight),
        in_specs=[anywhere] * 4,
        out_specs=(anywhere,) * 4,
        scratch_shapes=[
            pltpu.VMEM((3,) + latent_query.shape, BF16),
            pltpu.VMEM((4, 112, HD), BF16),
            pltpu.VMEM((112, 2, 2 * HD), F32),
            dma((3,)), dma((3,)), dma((2,)),
        ],
    )(*grads)


def solution(mesh):
    placed = (
        P("dp", ("seq", "tp"), None),
        P("dp", ("seq", "tp"), None),
        P("dp", ("seq", "tp"), None),
        P("dp", ("seq", "tp"), None),
        P("dp", None, None),
        P(None, None, "seq"),
    )
    return jax.shard_map(
        on_device,
        mesh=mesh,
        in_specs=placed,
        out_specs=(
            P("dp", ("seq", "tp"), None),
            P("dp", ("seq", "tp"), None),
            P("dp", ("seq", "tp"), None),
            P(("dp", "tp"), None, "seq"),
        ),
        check_vma=False,
    )
```

time: 76.9 us -> 73.5 us (0.956)
  Pallas kernels: 76.1 us -> 72.6 us
    pallas_call x1, Pallas kernels: 73.2 us -> 69.9 us  [on_device(): pl.pallas_call(kernel, name='attention_backward', out_shape=(token, token...]
where the time goes in v3:
time: 73.5 us; the launch traced here: 73.4 us
  Pallas kernels  72.6 us (99%)
  between operations  0.8 us (1%)
    pallas_call x1, Pallas kernels, on_device(): pl.pallas_call(kernel, name='attention_backward', out_shape=(token, token...  69.9 us
    pallas_call x1, Pallas kernels, on_device(): pl.pallas_call(place, name='place_outputs', out_shape=(token, token, toke...  2.63 us

profile of v3, /device:TPU:1, one launch (start us, length us, event | category | flops | bytes accessed | tf_op | source)
XLA Modules:
  0.0 73.4 jit_solution(4331617518570286855)
XLA Ops:
  0.6 69.9 %attention_backward.1 = (bf16[1,128,2048]{2,1,0:T(8,128)(2,1)}, bf16[1,128,2048]{2,1,0:T(8,128)(2,1)}, bf16[1,128,2048]{2,1,0:T(8,128)(2,1)}, bf16[4,112,128]{2,1,0:T(8,128)(2,1)}) custom-call(bf16[1,128,2048]{2,1,0:T(8,128)(2,1)} %lq.1, bf16[1,128,2048]{2,1,0:T(8,128)(2,1)} %lk.1, bf16[1,128,2048]{2,1,0:T(8,128)(2,1)} %lv.1, bf16[1,128,2048]{2,1,0:T(8,128)(2,1)} %og.1, ...), custom_call_target="tpu_custom_call" | custom-call | tf_op jit(solution)/shard_map/attention_backward/pallas_call | solution.py:488
  70.6 2.6 %place_outputs.1 = (bf16[1,128,2048]{2,1,0:T(8,128)(2,1)}, bf16[1,128,2048]{2,1,0:T(8,128)(2,1)}, bf16[1,128,2048]{2,1,0:T(8,128)(2,1)}, f32[112,2,256]{2,1,0:T(2,128)}) custom-call(bf16[1,128,2048]{2,1,0:T(8,128)(2,1)} %get-tuple-element.8.dq, bf16[1,128,2048]{2,1,0:T(8,128)(2,1)} %get-tuple-element.9.dk, bf16[1,128,2048]{2,1,0:T(8,128)(2,1)} %get-tuple-element.10.dv, ...), custom_call_target="tpu_custom_call" | custom-call | tf_op jit(solution)/shard_map/place_outputs/pallas_call | solution.py:535

commit v4 on v3

--- a/solution.py
+++ b/solution.py
@@ -10,7 +10,7 @@
 F32 = jnp.float32
 BF16 = jnp.bfloat16
 SCALE = HD ** (-0.5)
-SCALE2 = SCALE * 1.4426950408889634
+LOG2E = 1.4426950408889634
 ROWS = 128
 SLOTS = 16
 QB = 1024
@@ -22,6 +22,7 @@
 TILE_SLOTS = SLOTS // TILES
 BACK_TILES = KEYS // BT
 BACK_SLOTS = SLOTS // BACK_TILES
+KEPT = BACK_TILES - 2
 HALF_SLOTS = QB // ROWS
 GROUP = 4
 WINDOW = 512
@@ -64,8 +65,8 @@
 def kernel(
     lq, lk, lv, og, hidden, cw,
     dq_o, dk_o, dv_o, w_o,
-    qb, gb, kb, vb, qt, gt, qi, gi, e_s, dp_s, m_s, ka, va, dqa, dqb,
-    st, rx, fin, cwv, hid, hida, c_st, c_rx, cga, prod,
+    qb, gb, kb, vb, qt, gt, qi, gi, e_s, dp_s, dp_t, m_s, ka, va, dqa,
+    st, rx, cwv, hid, hida, c_st, c_rx, cga, prod,
     in_s, q_r, k_r, fw_s, fw_r, ex_s, ex_r, out_s, out_r,
     hid_s, hid_r, c1_s, c1_r, cg_s, cg_r, w_s, w_r, cw_sem, hid_sem,
 ):
@@ -139,8 +140,10 @@
                 in_copy(2 + a, src, dst, row, slot, k_r.at[a, slot // TILE_SLOTS]).start()
 
     with jax.named_scope("send_inputs"):
-        send_q(range(1, HALF_SLOTS))
-        send_k(range(1, SLOTS))
+        for slot in range(1, SLOTS):
+            if slot < HALF_SLOTS:
+                send_q([slot])
+            send_k([slot])
 
     def window(zz):
         return pl.ds(pl.multiple_of((7 * zz // 2) * HD, HD), WINDOW)
@@ -178,7 +181,10 @@
             with jax.named_scope("wait_queries"):
                 for a, dst in enumerate((qb, gb)):
                     arrived(dst.at[pl.ds(group * GROUP * ROWS, GROUP * ROWS)], q_r.at[a, group])
-        qt[half] = qb[pl.ds(half * QB, QB), :].T
+        scaled = qb[pl.ds(half * QB, QB), :].T.astype(F32) * (SCALE * LOG2E)
+        high = scaled.astype(BF16)
+        qt[half, :HD] = high
+        qt[half, HD:] = (scaled - high.astype(F32)).astype(BF16)
         gt[half] = gb[pl.ds(half * QB, QB), :].T
         dqa[half] = jnp.zeros((HD, QB), F32)
 
@@ -203,19 +209,20 @@
             for a, dst in enumerate((kb, vb)):
                 arrived(dst.at[pl.ds(0, TILE_SLOTS * ROWS)], fw_r.at[a, tile])
 
-    def forward(half, tile, stats, start, size):
+    def forward(half, tile, stats, start, size, kept=None):
         top, total, dots = stats
         keys = rows_at(start, size)
-        scores = mm(kb[keys, :], qt[half], 1, 0)
+        rows = kb[keys, :]
+        scores = mm(jnp.concatenate([rows, rows], 1), qt[half], 1, 0)
         dprobs = mm(vb[keys, :], gt[half], 1, 0)
-        top_new = jnp.maximum(top, jnp.ceil(jnp.max(scores, axis=0, keepdims=True) * SCALE2))
-        e = jnp.exp2(scores * SCALE2 - top_new)
+        top_new = jnp.maximum(top, jnp.ceil(jnp.max(scores, axis=0, keepdims=True)))
+        e = jnp.exp2(scores - top_new)
         shrink = jnp.exp2(top - top_new)
         total = total * shrink + jnp.sum(e, axis=0, keepdims=True)
         dots = dots * shrink + jnp.sum(e * dprobs, axis=0, keepdims=True)
         e_s[half, keys, :] = e.astype(BF16)
-        if half == 0:
-            dp_s[keys, :] = dprobs
+        if kept is not None:
+            kept[...] = dprobs
         m_s[half, pl.ds(tile, 1), :] = top_new
         return top_new, total, dots
 
@@ -223,10 +230,11 @@
         top, total, dots = stats
         inverse = 1.0 / total
         gi[half] = (gt[half].astype(F32) * inverse).astype(BF16)
-        qi[half] = (qt[half].astype(F32) * (inverse * SCALE)).astype(BF16)
+        both = qt[half, :HD].astype(F32) + qt[half, HD:].astype(F32)
+        qi[half] = (both * (inverse / LOG2E)).astype(BF16)
         return top, dots * inverse, inverse * SCALE
 
-    def backward(half, tile, stats, start, size, first=False, pair=False):
+    def backward(half, tile, stats, start, size, first=False, pair=False, kept=None):
         top, mean, _ = stats
         keys = rows_at(start, size)
         last = m_s[half, pl.ds(tile, 1), :]
@@ -238,7 +246,7 @@
         low = factor.astype(BF16)
         part_v = mm(e, gi[half] * low, 1, 1)
         va[keys, :] = part_v if first else va[keys, :] + part_v
-        dprobs = dp_s[keys, :] if half == 0 else mm(vb[keys, :], gt[half], 1, 0)
+        dprobs = mm(vb[keys, :], gt[half], 1, 0) if kept is None else kept[...]
         ds = (e.astype(F32) * (dprobs - mean)).astype(BF16)
         part_k = mm(ds, qi[half] * low, 1, 1)
         ka[keys, :] = part_k if first else ka[keys, :] + part_k
@@ -270,9 +278,9 @@
 
     def send_dq(half, stats):
         with jax.named_scope("send_dq"):
-            dqb[pl.ds(half * QB, QB), :] = (dqa[half] * stats[2]).T.astype(BF16)
+            qb[pl.ds(half * QB, QB), :] = (dqa[half] * stats[2]).T.astype(BF16)
             for slot in range(half * HALF_SLOTS, (half + 1) * HALF_SLOTS):
-                send_out(0, dqb.at[pl.ds(slot * ROWS, ROWS)], dq_o, slot)
+                send_out(0, qb.at[pl.ds(slot * ROWS, ROWS)], dq_o, slot)
 
     low = jnp.full((1, QB), -1e30, F32)
     zero = jnp.zeros((1, QB), F32)
@@ -283,32 +291,37 @@
         def _():
             pass_keys(tile + 1)
 
-        @pl.when(tile == 3)
+        @pl.when(tile == 2)
         def _():
             send_q(range(HALF_SLOTS, SLOTS))
 
         take_keys(tile)
         with jax.named_scope("forward_first"):
-            return forward(0, tile, stats, tile * KT, KT)
+            return forward(0, tile, stats, tile * KT, KT, dp_s.at[rows_at(tile * KT, KT)])
 
     take_queries(0)
-    first = forward(0, TILES, start, KEYS, COND)
+    first = forward(0, TILES, start, KEYS, COND, dp_s.at[pl.ds(KEYS, COND)])
     pass_keys(0)
     first = end_forward(0, lax.fori_loop(0, TILES, step_first, first))
 
     last = BACK_TILES - 1
     with jax.named_scope("backward_first"):
-        backward(0, TILES, first, KEYS, COND, True)
+        backward(0, TILES, first, KEYS, COND, True, kept=dp_s.at[pl.ds(KEYS, COND)])
         for tile in (last, last - 1):
-            backward(0, 2 * tile + 1, first, tile * BT, BT, True, True)
+            backward(0, 2 * tile + 1, first, tile * BT, BT, True, True, dp_s.at[rows_at(tile * BT, BT)])
 
     def step_second(tile, stats):
         with jax.named_scope("forward_second"):
             return forward(1, tile, stats, tile * BT, BT)
 
+    def step_kept(tile, stats):
+        with jax.named_scope("forward_second"):
+            return forward(1, tile, stats, tile * BT, BT, dp_t.at[rows_at((tile - KEPT) * BT, BT)])
+
     take_queries(1)
     second = forward(1, BACK_TILES, start, KEYS, COND)
-    second = end_forward(1, lax.fori_loop(0, BACK_TILES, step_second, second))
+    second = lax.fori_loop(0, KEPT, step_second, second)
+    second = end_forward(1, lax.fori_loop(KEPT, BACK_TILES, step_kept, second))
     backward(1, BACK_TILES, second, KEYS, COND)
 
     @pl.when(core == 0)
@@ -387,22 +400,27 @@
         with jax.named_scope("finish"):
             for a in range(2):
                 arrived(rx.at[a, pl.ds(slot, count)], ex_r.at[a, unit])
-            for i in range(count):
-                mine = rows_at((slot + i) * 2 * ROWS + core * ROWS, ROWS)
-                for a, (acc, dst) in enumerate(((ka, dk_o), (va, dv_o))):
-                    fin[a, slot + i] = (acc[mine, :] + rx[a, slot + i].astype(F32)).astype(BF16)
-                    send_out(1 + a, fin.at[a, slot + i], dst, slot + i)
+            for a, (acc, dst) in enumerate(((ka, dk_o), (va, dv_o))):
+                for i in range(count):
+                    mine = rows_at((slot + i) * 2 * ROWS + core * ROWS, ROWS)
+                    rx[a, slot + i] = (acc[mine, :] + rx[a, slot + i].astype(F32)).astype(BF16)
+                    send_out(1 + a, rx.at[a, slot + i], dst, slot + i)
 
     for unit in range(2):
         with jax.named_scope("backward_tile"):
-            backward(1, last, second, last * BT + unit * KT, KT)
+            backward(
+                1, last, second, last * BT + unit * KT, KT,
+                kept=dp_t.at[pl.ds((last - KEPT) * BT + unit * KT, KT)],
+            )
         swap(unit, last * BACK_SLOTS + unit * 2, 2)
     with jax.named_scope("condition_sum"):
         cond_sum()
     finish(0, last * BACK_SLOTS, 2)
 
     with jax.named_scope("backward_tile"):
-        backward(1, last - 1, second, (last - 1) * BT, BT)
+        backward(
+            1, last - 1, second, (last - 1) * BT, BT, kept=dp_t.at[pl.ds((last - 1 - KEPT) * BT, BT)]
+        )
     swap(2, (last - 1) * BACK_SLOTS, BACK_SLOTS)
     finish(1, last * BACK_SLOTS + 2, 2)
 
@@ -415,14 +433,14 @@
         def _():
             send_dq(1, second)
 
-        @pl.when(step == 2)
+        @pl.when(tile == 0)
         def _():
             with jax.named_scope("condition_product"):
                 cond_product()
 
         finish(step, (tile + 1) * BACK_SLOTS, BACK_SLOTS)
         with jax.named_scope("backward_tile"):
-            backward(0, 2 * tile + 1, first, tile * BT, BT, False, True)
+            backward(0, 2 * tile + 1, first, tile * BT, BT, False, True, dp_s.at[rows_at(tile * BT, BT)])
         swap(step + 1, tile * BACK_SLOTS, BACK_SLOTS)
         return carry
 
@@ -441,7 +459,7 @@
         arrived(hida.at[pl.ds(1, 7)], hid_s)
         arrived(cga.at[pl.ds(1, 7)], cg_s)
         for a in range(3):
-            arrived(dqb.at[sent], out_s.at[a])
+            arrived(qb.at[sent], out_s.at[a])
     with jax.named_scope("drain_weight"):
         arrived(w_o.at[pl.ds(0, 3)], w_s)
         arrived(w_o, w_r)
@@ -496,18 +514,17 @@
             pltpu.VMEM((2 * QB, HD), BF16),
             pltpu.VMEM((total_keys, HD), BF16),
             pltpu.VMEM((total_keys, HD), BF16),
-            pltpu.VMEM((2, HD, QB), BF16),
+            pltpu.VMEM((2, 2 * HD, QB), BF16),
             pltpu.VMEM((2, HD, QB), BF16),
             pltpu.VMEM((2, HD, QB), BF16),
             pltpu.VMEM((2, HD, QB), BF16),
             pltpu.VMEM((2, total_keys, QB), BF16),
             pltpu.VMEM((total_keys, QB), F32),
+            pltpu.VMEM(((BACK_TILES - KEPT) * BT, QB), F32),
             pltpu.VMEM((2, 16, QB), F32),
             pltpu.VMEM((total_keys, HD), F32),
             pltpu.VMEM((total_keys, HD), F32),
             pltpu.VMEM((2, HD, QB), F32),
-            pltpu.VMEM((2 * QB, HD), BF16),
-            pltpu.VMEM((2, SLOTS, ROWS, HD), BF16),
             pltpu.VMEM((2, SLOTS, ROWS, HD), BF16),
             pltpu.VMEM((2, SLOTS, ROWS, HD), BF16),
             pltpu.VMEM((cond_weight.shape[0], 2, HD), BF16),
@@ -528,7 +545,7 @@
             dma, dma,
         ],
         compiler_params=pltpu.CompilerParams(
-            collective_id=0, has_side_effects=True, vmem_limit_bytes=60 << 20
+            collective_id=0, has_side_effects=True, vmem_limit_bytes=63 << 20
         ),
     )(latent_query, latent_key, latent_value, out_grad, query_hidden, cond_weight)
     weight = jax.ShapeDtypeStruct((112, 2, 2 * HD), F32)

time: 73.5 us -> 72.9 us (level)
  no operation moved by 1% of the time
where the time goes in v4:
time: 72.9 us; the launch traced here: 72.7 us
  Pallas kernels  71.9 us (99%)
  between operations  0.8 us (1%)
    pallas_call x1, Pallas kernels, on_device(): pl.pallas_call(kernel, name='attention_backward', out_shape=(token, token...  69.3 us
    pallas_call x1, Pallas kernels, on_device(): pl.pallas_call(place, name='place_outputs', out_shape=(token, token, toke...  2.63 us

profile of v4, /device:TPU:1, one launch (start us, length us, event | category | flops | bytes accessed | tf_op | source)
XLA Modules:
  0.0 72.7 jit_solution(16166969683239865687)
XLA Ops:
  0.6 69.3 %attention_backward.1 = (bf16[1,128,2048]{2,1,0:T(8,128)(2,1)}, bf16[1,128,2048]{2,1,0:T(8,128)(2,1)}, bf16[1,128,2048]{2,1,0:T(8,128)(2,1)}, bf16[4,112,128]{2,1,0:T(8,128)(2,1)}) custom-call(bf16[1,128,2048]{2,1,0:T(8,128)(2,1)} %lq.1, bf16[1,128,2048]{2,1,0:T(8,128)(2,1)} %lk.1, bf16[1,128,2048]{2,1,0:T(8,128)(2,1)} %lv.1, bf16[1,128,2048]{2,1,0:T(8,128)(2,1)} %og.1, ...), custom_call_target="tpu_custom_call" | custom-call | tf_op jit(solution)/shard_map/attention_backward/pallas_call | solution.py:506
  69.9 2.6 %place_outputs.1 = (bf16[1,128,2048]{2,1,0:T(8,128)(2,1)}, bf16[1,128,2048]{2,1,0:T(8,128)(2,1)}, bf16[1,128,2048]{2,1,0:T(8,128)(2,1)}, f32[112,2,256]{2,1,0:T(2,128)}) custom-call(bf16[1,128,2048]{2,1,0:T(8,128)(2,1)} %get-tuple-element.8.dq, bf16[1,128,2048]{2,1,0:T(8,128)(2,1)} %get-tuple-element.9.dk, bf16[1,128,2048]{2,1,0:T(8,128)(2,1)} %get-tuple-element.10.dv, ...), custom_call_target="tpu_custom_call" | custom-call | tf_op jit(solution)/shard_map/place_outputs/pallas_call | solution.py:552

commit v5 on v4

--- a/solution.py
+++ b/solution.py
@@ -13,7 +13,8 @@
 LOG2E = 1.4426950408889634
 ROWS = 128
 SLOTS = 16
-QB = 1024
+HALF_SLOTS = 10
+QB = (HALF_SLOTS * ROWS, (SLOTS - HALF_SLOTS) * ROWS)
 KT = 512
 BT = 2 * KT
 KEYS = 4096
@@ -22,9 +23,8 @@
 TILE_SLOTS = SLOTS // TILES
 BACK_TILES = KEYS // BT
 BACK_SLOTS = SLOTS // BACK_TILES
-KEPT = BACK_TILES - 2
-HALF_SLOTS = QB // ROWS
-GROUP = 4
+KEPT = BACK_TILES - 1
+GROUP = 2
 WINDOW = 512
 
 
@@ -65,11 +65,13 @@
 def kernel(
     lq, lk, lv, og, hidden, cw,
     dq_o, dk_o, dv_o, w_o,
-    qb, gb, kb, vb, qt, gt, qi, gi, e_s, dp_s, dp_t, m_s, ka, va, dqa,
+    qb, gb, kb, vb, qt0, qt1, gt0, gt1, qi0, qi1, gi0, gi1, e0, e1, dp_s, dp_t, m0, m1, ka, va, dqa0, dqa1,
     st, rx, cwv, hid, hida, c_st, c_rx, cga, prod,
     in_s, q_r, k_r, fw_s, fw_r, ex_s, ex_r, out_s, out_r,
     hid_s, hid_r, c1_s, c1_r, cg_s, cg_r, w_s, w_r, cw_sem, hid_sem,
 ):
+    qt, gt, qi, gi = (qt0, qt1), (gt0, gt1), (qi0, qi1), (gi0, gi1)
+    e_s, m_s, dqa = (e0, e1), (m0, m1), (dqa0, dqa1)
     z = lax.axis_index("dp")
     seq = lax.axis_index("seq")
     tp = lax.axis_index("tp")
@@ -176,17 +178,23 @@
     kb[pl.ds(KEYS, COND), :] = cond_k.astype(BF16)
     vb[pl.ds(KEYS, COND), :] = cond_v.astype(BF16)
 
+    def slots_of(half):
+        return range(HALF_SLOTS) if half == 0 else range(HALF_SLOTS, SLOTS)
+
+    def rows_of(half):
+        return pl.ds(half * QB[0], QB[half])
+
     def take_queries(half):
-        for group in (2 * half, 2 * half + 1):
+        for group in range(slots_of(half)[0] // GROUP, (slots_of(half)[-1] + 1) // GROUP):
             with jax.named_scope("wait_queries"):
                 for a, dst in enumerate((qb, gb)):
                     arrived(dst.at[pl.ds(group * GROUP * ROWS, GROUP * ROWS)], q_r.at[a, group])
-        scaled = qb[pl.ds(half * QB, QB), :].T.astype(F32) * (SCALE * LOG2E)
+        scaled = qb[rows_of(half), :].T.astype(F32) * (SCALE * LOG2E)
         high = scaled.astype(BF16)
-        qt[half, :HD] = high
-        qt[half, HD:] = (scaled - high.astype(F32)).astype(BF16)
-        gt[half] = gb[pl.ds(half * QB, QB), :].T
-        dqa[half] = jnp.zeros((HD, QB), F32)
+        qt[half][:HD, :] = high
+        qt[half][HD:, :] = (scaled - high.astype(F32)).astype(BF16)
+        gt[half][...] = gb[rows_of(half), :].T
+        dqa[half][...] = jnp.zeros((HD, QB[half]), F32)
 
     def pass_keys(tile):
         with jax.named_scope("wait_keys"):
@@ -213,44 +221,44 @@
         top, total, dots = stats
         keys = rows_at(start, size)
         rows = kb[keys, :]
-        scores = mm(jnp.concatenate([rows, rows], 1), qt[half], 1, 0)
-        dprobs = mm(vb[keys, :], gt[half], 1, 0)
+        scores = mm(jnp.concatenate([rows, rows], 1), qt[half][...], 1, 0)
+        dprobs = mm(vb[keys, :], gt[half][...], 1, 0)
         top_new = jnp.maximum(top, jnp.ceil(jnp.max(scores, axis=0, keepdims=True)))
         e = jnp.exp2(scores - top_new)
         shrink = jnp.exp2(top - top_new)
         total = total * shrink + jnp.sum(e, axis=0, keepdims=True)
         dots = dots * shrink + jnp.sum(e * dprobs, axis=0, keepdims=True)
-        e_s[half, keys, :] = e.astype(BF16)
+        e_s[half][keys, :] = e.astype(BF16)
         if kept is not None:
             kept[...] = dprobs
-        m_s[half, pl.ds(tile, 1), :] = top_new
+        m_s[half][pl.ds(tile, 1), :] = top_new
         return top_new, total, dots
 
     def end_forward(half, stats):
         top, total, dots = stats
         inverse = 1.0 / total
-        gi[half] = (gt[half].astype(F32) * inverse).astype(BF16)
-        both = qt[half, :HD].astype(F32) + qt[half, HD:].astype(F32)
-        qi[half] = (both * (inverse / LOG2E)).astype(BF16)
+        gi[half][...] = (gt[half][...].astype(F32) * inverse).astype(BF16)
+        both = qt[half][:HD, :].astype(F32) + qt[half][HD:, :].astype(F32)
+        qi[half][...] = (both * (inverse / LOG2E)).astype(BF16)
         return top, dots * inverse, inverse * SCALE
 
     def backward(half, tile, stats, start, size, first=False, pair=False, kept=None):
         top, mean, _ = stats
         keys = rows_at(start, size)
-        last = m_s[half, pl.ds(tile, 1), :]
-        e = e_s[half, keys, :]
+        last = m_s[half][pl.ds(tile, 1), :]
+        e = e_s[half][keys, :]
         if pair:
-            step = jnp.exp2(m_s[half, pl.ds(tile - 1, 1), :] - last).astype(BF16)
+            step = jnp.exp2(m_s[half][pl.ds(tile - 1, 1), :] - last).astype(BF16)
             e = jnp.concatenate([e[: size // 2] * step, e[size // 2 :]], 0)
         factor = jnp.exp2(last - top)
         low = factor.astype(BF16)
-        part_v = mm(e, gi[half] * low, 1, 1)
+        part_v = mm(e, gi[half][...] * low, 1, 1)
         va[keys, :] = part_v if first else va[keys, :] + part_v
-        dprobs = mm(vb[keys, :], gt[half], 1, 0) if kept is None else kept[...]
+        dprobs = mm(vb[keys, :], gt[half][...], 1, 0) if kept is None else kept[...]
         ds = (e.astype(F32) * (dprobs - mean)).astype(BF16)
-        part_k = mm(ds, qi[half] * low, 1, 1)
+        part_k = mm(ds, qi[half][...] * low, 1, 1)
         ka[keys, :] = part_k if first else ka[keys, :] + part_k
-        dqa[half] += mm(kb[keys, :], ds, 0, 0) * factor
+        dqa[half][...] += mm(kb[keys, :], ds, 0, 0) * factor
 
     def out_copy(a, src, dst, slot):
         device, _ = chip(slot, -1)
@@ -278,13 +286,13 @@
 
     def send_dq(half, stats):
         with jax.named_scope("send_dq"):
-            qb[pl.ds(half * QB, QB), :] = (dqa[half] * stats[2]).T.astype(BF16)
-            for slot in range(half * HALF_SLOTS, (half + 1) * HALF_SLOTS):
+            qb[rows_of(half), :] = (dqa[half][...] * stats[2]).T.astype(BF16)
+            for slot in slots_of(half):
                 send_out(0, qb.at[pl.ds(slot * ROWS, ROWS)], dq_o, slot)
 
-    low = jnp.full((1, QB), -1e30, F32)
-    zero = jnp.zeros((1, QB), F32)
-    start = (low, zero, zero)
+    def start(half):
+        zero = jnp.zeros((1, QB[half]), F32)
+        return zero - 1e30, zero, zero
 
     def step_first(tile, stats):
         @pl.when(tile < TILES - 1)
@@ -300,7 +308,7 @@
             return forward(0, tile, stats, tile * KT, KT, dp_s.at[rows_at(tile * KT, KT)])
 
     take_queries(0)
-    first = forward(0, TILES, start, KEYS, COND, dp_s.at[pl.ds(KEYS, COND)])
+    first = forward(0, TILES, start(0), KEYS, COND, dp_s.at[pl.ds(KEYS, COND)])
     pass_keys(0)
     first = end_forward(0, lax.fori_loop(0, TILES, step_first, first))
 
@@ -319,22 +327,9 @@
             return forward(1, tile, stats, tile * BT, BT, dp_t.at[rows_at((tile - KEPT) * BT, BT)])
 
     take_queries(1)
-    second = forward(1, BACK_TILES, start, KEYS, COND)
+    second = forward(1, BACK_TILES, start(1), KEYS, COND)
     second = lax.fori_loop(0, KEPT, step_second, second)
     second = end_forward(1, lax.fori_loop(KEPT, BACK_TILES, step_kept, second))
-    backward(1, BACK_TILES, second, KEYS, COND)
-
-    @pl.when(core == 0)
-    def _():
-        c_st[...] = va[pl.ds(KEYS, COND), :].astype(BF16)
-
-    @pl.when(core == 1)
-    def _():
-        c_st[...] = ka[pl.ds(KEYS, COND), :].astype(BF16)
-
-    pltpu.make_async_remote_copy(
-        src_ref=c_st, dst_ref=c_rx, send_sem=c1_s, recv_sem=c1_r, device_id=partner, device_id_type=MESH
-    ).start()
 
     def cond_sum():
         arrived(c_rx, c1_r)
@@ -406,21 +401,36 @@
                     rx[a, slot + i] = (acc[mine, :] + rx[a, slot + i].astype(F32)).astype(BF16)
                     send_out(1 + a, rx.at[a, slot + i], dst, slot + i)
 
-    for unit in range(2):
+    def first_tile(unit):
         with jax.named_scope("backward_tile"):
             backward(
                 1, last, second, last * BT + unit * KT, KT,
                 kept=dp_t.at[pl.ds((last - KEPT) * BT + unit * KT, KT)],
             )
         swap(unit, last * BACK_SLOTS + unit * 2, 2)
+
+    first_tile(0)
+    backward(1, BACK_TILES, second, KEYS, COND)
+
+    @pl.when(core == 0)
+    def _():
+        c_st[...] = va[pl.ds(KEYS, COND), :].astype(BF16)
+
+    @pl.when(core == 1)
+    def _():
+        c_st[...] = ka[pl.ds(KEYS, COND), :].astype(BF16)
+
+    pltpu.make_async_remote_copy(
+        src_ref=c_st, dst_ref=c_rx, send_sem=c1_s, recv_sem=c1_r, device_id=partner, device_id_type=MESH
+    ).start()
+
+    first_tile(1)
+    finish(0, last * BACK_SLOTS, 2)
     with jax.named_scope("condition_sum"):
         cond_sum()
-    finish(0, last * BACK_SLOTS, 2)
 
     with jax.named_scope("backward_tile"):
-        backward(
-            1, last - 1, second, (last - 1) * BT, BT, kept=dp_t.at[pl.ds((last - 1 - KEPT) * BT, BT)]
-        )
+        backward(1, last - 1, second, (last - 1) * BT, BT)
     swap(2, (last - 1) * BACK_SLOTS, BACK_SLOTS)
     finish(1, last * BACK_SLOTS + 2, 2)
 
@@ -510,21 +520,19 @@
         in_specs=[anywhere] * 6,
         out_specs=(anywhere,) * 4,
         scratch_shapes=[
-            pltpu.VMEM((2 * QB, HD), BF16),
-            pltpu.VMEM((2 * QB, HD), BF16),
+            pltpu.VMEM((SLOTS * ROWS, HD), BF16),
+            pltpu.VMEM((SLOTS * ROWS, HD), BF16),
             pltpu.VMEM((total_keys, HD), BF16),
             pltpu.VMEM((total_keys, HD), BF16),
-            pltpu.VMEM((2, 2 * HD, QB), BF16),
-            pltpu.VMEM((2, HD, QB), BF16),
-            pltpu.VMEM((2, HD, QB), BF16),
-            pltpu.VMEM((2, HD, QB), BF16),
-            pltpu.VMEM((2, total_keys, QB), BF16),
-            pltpu.VMEM((total_keys, QB), F32),
-            pltpu.VMEM(((BACK_TILES - KEPT) * BT, QB), F32),
-            pltpu.VMEM((2, 16, QB), F32),
+            *(pltpu.VMEM((2 * HD, n), BF16) for n in QB),
+            *(pltpu.VMEM((HD, n), BF16) for n in QB * 3),
+            *(pltpu.VMEM((total_keys, n), BF16) for n in QB),
+            pltpu.VMEM((total_keys, QB[0]), F32),
+            pltpu.VMEM(((BACK_TILES - KEPT) * BT, QB[1]), F32),
+            *(pltpu.VMEM((16, n), F32) for n in QB),
             pltpu.VMEM((total_keys, HD), F32),
             pltpu.VMEM((total_keys, HD), F32),
-            pltpu.VMEM((2, HD, QB), F32),
+            *(pltpu.VMEM((HD, n), F32) for n in QB),
             pltpu.VMEM((2, SLOTS, ROWS, HD), BF16),
             pltpu.VMEM((2, SLOTS, ROWS, HD), BF16),
             pltpu.VMEM((cond_weight.shape[0], 2, HD), BF16),

time: 72.9 us -> 72.2 us (level)
  no operation moved by 1% of the time
where the time goes in v5:
time: 72.2 us; the launch traced here: 72.1 us
  Pallas kernels  71.3 us (99%)
  between operations  0.8 us (1%)
    pallas_call x1, Pallas kernels, on_device(): pl.pallas_call(kernel, name='attention_backward', out_shape=(token, token...  68.7 us
    pallas_call x1, Pallas kernels, on_device(): pl.pallas_call(place, name='place_outputs', out_shape=(token, token, toke...  2.63 us

profile of v5, /device:TPU:1, one launch (start us, length us, event | category | flops | bytes accessed | tf_op | source)
XLA Modules:
  0.0 72.1 jit_solution(725103569938913359)
XLA Ops:
  0.6 68.7 %attention_backward.1 = (bf16[1,128,2048]{2,1,0:T(8,128)(2,1)}, bf16[1,128,2048]{2,1,0:T(8,128)(2,1)}, bf16[1,128,2048]{2,1,0:T(8,128)(2,1)}, bf16[4,112,128]{2,1,0:T(8,128)(2,1)}) custom-call(bf16[1,128,2048]{2,1,0:T(8,128)(2,1)} %lq.1, bf16[1,128,2048]{2,1,0:T(8,128)(2,1)} %lk.1, bf16[1,128,2048]{2,1,0:T(8,128)(2,1)} %lv.1, bf16[1,128,2048]{2,1,0:T(8,128)(2,1)} %og.1, ...), custom_call_target="tpu_custom_call" | custom-call | tf_op jit(solution)/shard_map/attention_backward/pallas_call | solution.py:516
  69.3 2.6 %place_outputs.1 = (bf16[1,128,2048]{2,1,0:T(8,128)(2,1)}, bf16[1,128,2048]{2,1,0:T(8,128)(2,1)}, bf16[1,128,2048]{2,1,0:T(8,128)(2,1)}, f32[112,2,256]{2,1,0:T(2,128)}) custom-call(bf16[1,128,2048]{2,1,0:T(8,128)(2,1)} %get-tuple-element.8.dq, bf16[1,128,2048]{2,1,0:T(8,128)(2,1)} %get-tuple-element.9.dk, bf16[1,128,2048]{2,1,0:T(8,128)(2,1)} %get-tuple-element.10.dv, ...), custom_call_target="tpu_custom_call" | custom-call | tf_op jit(solution)/shard_map/place_outputs/pallas_call | solution.py:560

commit v6 on v5

--- a/solution.py
+++ b/solution.py
@@ -113,7 +113,7 @@
         pltpu.make_async_copy(src.at[0, :, feat(head)], dst.at[pl.ds(0, ROWS)], q_r.at[a, 0]).start()
     for a, (src, dst) in enumerate(((lk, kb), (lv, vb))):
         pltpu.make_async_copy(
-            src.at[0, :, feat(head)], dst.at[rows_at(core * ROWS, ROWS)], k_r.at[a, 0]
+            src.at[0, :, feat(head)], dst.at[rows_at(core * ROWS, ROWS)], k_r.at[0]
         ).start()
 
     with jax.named_scope("barrier"):
@@ -133,13 +133,13 @@
     def send_q(slots):
         for slot in slots:
             for a, (src, dst) in enumerate(((lq, qb), (og, gb))):
-                in_copy(a, src, dst, slot * ROWS, slot, q_r.at[a, slot // GROUP]).start()
+                in_copy(a, src, dst, slot * ROWS, slot, q_r.at[a, slot // HALF_SLOTS]).start()
 
     def send_k(slots):
         for slot in slots:
             row = slot * 2 * ROWS + core * ROWS
             for a, (src, dst) in enumerate(((lk, kb), (lv, vb))):
-                in_copy(2 + a, src, dst, row, slot, k_r.at[a, slot // TILE_SLOTS]).start()
+                in_copy(2 + a, src, dst, row, slot, k_r.at[slot // TILE_SLOTS]).start()
 
     with jax.named_scope("send_inputs"):
         for slot in range(1, SLOTS):
@@ -185,10 +185,9 @@
         return pl.ds(half * QB[0], QB[half])
 
     def take_queries(half):
-        for group in range(slots_of(half)[0] // GROUP, (slots_of(half)[-1] + 1) // GROUP):
-            with jax.named_scope("wait_queries"):
-                for a, dst in enumerate((qb, gb)):
-                    arrived(dst.at[pl.ds(group * GROUP * ROWS, GROUP * ROWS)], q_r.at[a, group])
+        with jax.named_scope("wait_queries"):
+            for a, dst in enumerate((qb, gb)):
+                arrived(dst.at[rows_of(half)], q_r.at[a, half])
         scaled = qb[rows_of(half), :].T.astype(F32) * (SCALE * LOG2E)
         high = scaled.astype(BF16)
         qt[half][:HD, :] = high
@@ -198,8 +197,7 @@
 
     def pass_keys(tile):
         with jax.named_scope("wait_keys"):
-            for a, dst in enumerate((kb, vb)):
-                arrived(dst.at[pl.ds(0, TILE_SLOTS * ROWS)], k_r.at[a, tile])
+            arrived(kb.at[pl.ds(0, 2 * TILE_SLOTS * ROWS)], k_r.at[tile])
         for i in range(TILE_SLOTS):
             for a, dst in enumerate((kb, vb)):
                 mine = dst.at[rows_at((tile * TILE_SLOTS + i) * 2 * ROWS + core * ROWS, ROWS)]
@@ -207,15 +205,14 @@
                     src_ref=mine,
                     dst_ref=mine,
                     send_sem=fw_s.at[a],
-                    recv_sem=fw_r.at[a, tile],
+                    recv_sem=fw_r.at[tile],
                     device_id=partner,
                     device_id_type=MESH,
                 ).start()
 
     def take_keys(tile):
         with jax.named_scope("wait_partner_keys"):
-            for a, dst in enumerate((kb, vb)):
-                arrived(dst.at[pl.ds(0, TILE_SLOTS * ROWS)], fw_r.at[a, tile])
+            arrived(kb.at[pl.ds(0, 2 * TILE_SLOTS * ROWS)], fw_r.at[tile])
 
     def forward(half, tile, stats, start, size, kept=None):
         top, total, dots = stats
@@ -542,8 +539,8 @@
             pltpu.VMEM((COND, HD), BF16),
             pltpu.VMEM((8, COND, HD), BF16),
             pltpu.VMEM((WINDOW, HD), BF16),
-            dma((4,)), dma((2, SLOTS // GROUP)), dma((2, TILES)),
-            dma((2,)), dma((2, TILES)),
+            dma((4,)), dma((2, 2)), dma((TILES,)),
+            dma((2,)), dma((TILES,)),
             dma((2,)), dma((2, BACK_TILES + 1)),
             dma((3,)), dma((3,)),
             dma, dma,

time: 72.2 us -> 72 us (level)
  no operation moved by 1% of the time
where the time goes in v6:
time: 72 us; the launch traced here: 71.8 us
  Pallas kernels  71 us (99%)
  between operations  0.8 us (1%)
    pallas_call x1, Pallas kernels, on_device(): pl.pallas_call(kernel, name='attention_backward', out_shape=(token, token...  68.4 us
    pallas_call x1, Pallas kernels, on_device(): pl.pallas_call(place, name='place_outputs', out_shape=(token, token, toke...  2.63 us

profile of v6, /device:TPU:1, one launch (start us, length us, event | category | flops | bytes accessed | tf_op | source)
XLA Modules:
  0.0 71.8 jit_solution(5881043225610602789)
XLA Ops:
  0.6 68.4 %attention_backward.1 = (bf16[1,128,2048]{2,1,0:T(8,128)(2,1)}, bf16[1,128,2048]{2,1,0:T(8,128)(2,1)}, bf16[1,128,2048]{2,1,0:T(8,128)(2,1)}, bf16[4,112,128]{2,1,0:T(8,128)(2,1)}) custom-call(bf16[1,128,2048]{2,1,0:T(8,128)(2,1)} %lq.1, bf16[1,128,2048]{2,1,0:T(8,128)(2,1)} %lk.1, bf16[1,128,2048]{2,1,0:T(8,128)(2,1)} %lv.1, bf16[1,128,2048]{2,1,0:T(8,128)(2,1)} %og.1, ...), custom_call_target="tpu_custom_call" | custom-call | tf_op jit(solution)/shard_map/attention_backward/pallas_call | solution.py:513
  69.0 2.6 %place_outputs.1 = (bf16[1,128,2048]{2,1,0:T(8,128)(2,1)}, bf16[1,128,2048]{2,1,0:T(8,128)(2,1)}, bf16[1,128,2048]{2,1,0:T(8,128)(2,1)}, f32[112,2,256]{2,1,0:T(2,128)}) custom-call(bf16[1,128,2048]{2,1,0:T(8,128)(2,1)} %get-tuple-element.8.dq, bf16[1,128,2048]{2,1,0:T(8,128)(2,1)} %get-tuple-element.9.dk, bf16[1,128,2048]{2,1,0:T(8,128)(2,1)} %get-tuple-element.10.dv, ...), custom_call_target="tpu_custom_call" | custom-call | tf_op jit(solution)/shard_map/place_outputs/pallas_call | solution.py:557
